TPU v7x, 32 devices: a whole 2x2x4 slice. The times are simulated.
32 devices in a mesh: groups: 2 (over x), ab: 8 (over z, y), cd: 2 (over core).
Axes of the slice: x: 2, y: 2, z: 4, core: 2. Of those that a mesh axis runs over, the one named last changes fastest.
Arguments:
- amplitudes: float32 [4, 128, 4096], P('groups', 'ab', 'cd'), parts along dimension 0, may hold values from -6 to 6
- integrals: float32 [16384, 4096], P(('groups', 'ab'), 'cd'), parts along dimension 0, may hold values from -0.21875 to 0.21875
- ab_irrep: int32 [128], P(('groups', 'ab')), parts along dimension 0, may hold values from 0 to 7
- cd_irrep: int32 [64], P(('groups', 'cd')), parts along dimension 0, may hold values from 0 to 7
- block_pattern: int32 [128, 32], P(('groups', 'ab'), 'cd'), parts along dimension 0, may hold values 0 or 1
Outputs:
- residual: float32 [4, 128, 8192], P('groups', 'cd', 'ab'), parts along dimension 0
There are 2 independent parts, one for each index of `groups`. A program takes and returns all parts, laid end to end along the dimension named above; each array names one. Nothing has to cross between parts.
All inputs are finite; a program needn't handle non-finite values. No bound on the sum of `block_pattern` on one device may be relied on, other than what follows from the above.
Results may differ from a plain program's by a relative error of at most 0.000071.
Values sent between devices are 32-bit elements; how exact they have to be, the bound alone decides.
No kernel may reach another device: no remote copies, remote signals or barrier semaphores. Data moves between devices by JAX's collectives and lax.ppermute only.
A program may use at most 128 MiB of HBM per device.

v0:
```python
import jax
import jax.numpy as jnp
from jax import lax
from jax.sharding import PartitionSpec as P

TILE = 128


def shards(amplitudes, integrals, ab_irrep, cd_irrep, block_pattern):
    ab_count = ab_irrep.shape[0]
    cd_count = cd_irrep.shape[0]
    allowed = ((block_pattern == 1) & (ab_irrep[:, None] == cd_irrep[None, :])).astype(jnp.float32)
    masked = (
        integrals.reshape(ab_count, TILE, cd_count, TILE) * allowed[:, None, :, None]
    ).reshape(integrals.shape)
    piece = lax.all_gather(amplitudes, "ab", axis=1, tiled=True)
    terms = lax.dot_general(
        piece,
        masked,
        (((piece.ndim - 1,), (1,)), ((), ())),
        precision=lax.Precision.HIGHEST,
        preferred_element_type=jnp.float32,
    )
    return lax.psum_scatter(terms, "cd", scatter_dimension=1, tiled=True)


def solution(mesh):
    in_specs = (
        P("groups", "ab", "cd"),
        P(("groups", "ab"), "cd"),
        P(("groups", "ab")),
        P(("groups", "cd")),
        P(("groups", "ab"), "cd"),
    )
    out_specs = P("groups", "cd", "ab")
    return jax.shard_map(shards, mesh=mesh, in_specs=in_specs, out_specs=out_specs, check_vma=False)
```

profile of v0, /device:TPU:1, one launch (start us, length us, event | category | flops | bytes accessed | tf_op | source)
XLA Modules:
  0.0 103.4 jit_solution(9463183384200436592)
XLA Ops:
  6.5 0.0 all-gather.2.cloned.1.call-start
  6.5 0.7 all-gather.2.cloned.1.call-update
  7.3 0.0 all-reduce.3.cloned.1.call-start
  7.3 0.8 and_convert_fusion
  8.1 51.7 %all-gather.2.cloned.1.call-done = f32[2,128,2048]{2,1,0:T(8,128)} async-done(((f32[2,16,2048]{2,1,0:T(8,128)}), f32[2,128,2048]{2,1,0:T(8,128)}) %all-gather.2.cloned.1.call-update) | async-done | bytes 2097168 | tf_op jit(solution)/shard_map/all_gather | solution.py:16
  59.8 0.0 copy-start
  59.8 0.6 mul.11
  60.4 2.8 %copy-done = f32[1024,2048]{1,0:T(8,128)S(1)} copy-done((f32[1024,2048]{1,0:T(8,128)S(1)}, f32[1024,2048]{1,0:T(8,128)}, u32[]{:S(2)}) %copy-start) | copy-done | bytes 8388632
  63.2 0.0 copy-start.1
  63.2 10.2 %fusion.4 = f32[2,128,1024]{1,2,0:T(8,128)S(1)} fusion(f32[2,128,2048]{2,1,0:T(8,128)} %all-gather.2.cloned.1.call-done, f32[1024,2048]{1,0:T(8,128)S(1)} %copy-done, f32[128,8,16,128]{3,2,1,0:T(8,128)S(1)} %bitcast.18), kind=kOutput, calls=%fused_computation.4 | convolution fusion | flops 6444548096 | bytes 19922944 | tf_op jit(solution)/shard_map/dot_general | solution.py:17
  73.4 1.3 %copy.7 = f32[2,128,1024]{2,0,1:T(2,128)} copy(f32[2,128,1024]{1,2,0:T(8,128)S(1)} %fusion.4) | data formatting | bytes 2097152 | tf_op jit(solution)/shard_map/dot_general | solution.py:17
  74.7 0.0 all-reduce.3.cloned.1.call-update
  74.8 0.0 copy-done.1
  74.8 0.6 dynamic-slice
  76.0 18.5 %all-reduce.3.cloned.1.call-done = f32[2,128,1024]{2,0,1:T(2,128)} async-done(((f32[2,128,1024]{2,0,1:T(2,128)}), f32[2,128,1024]{2,0,1:T(2,128)}) %all-reduce.3.cloned.1.call-update) | async-done | bytes 1048592
  94.5 1.1 %constant_dynamic-slice_fusion = f32[2,64,1024]{2,0,1:T(2,128)S(1)} fusion(f32[2,128,1024]{2,0,1:T(2,128)} %all-reduce.3.cloned.1.call-done, u32[]{:T(128)S(6)} %multiply.1), kind=kLoop, calls=%fused_computation.6 | loop fusion | bytes 1048580
  95.6 1.0 copy.8
Async XLA Ops:
  6.5 53.3 %all-gather.2.cloned.1.call-start = ((), (), s32[]{:S(2)}) async-start(), calls=%async_computation | async-start | bytes 2359296 | tf_op jit(solution)/shard_map/all_gather | solution.py:16
  7.3 87.2 %all-reduce.3.cloned.1.call-start = ((), (), s32[]{:S(2)}) async-start(), calls=%async_computation.1 | async-start | bytes 2097152
  59.8 3.4 %copy-start = (f32[1024,2048]{1,0:T(8,128)S(1)}, f32[1024,2048]{1,0:T(8,128)}, u32[]{:S(2)}) copy-start(f32[1024,2048]{1,0:T(8,128)} %param.6) | copy-start | bytes 25165828
  63.2 11.6 %copy-start.1 = (u32[32]{0:T(128)S(1)}, u32[32]{0:T(128)}, u32[]{:S(2)}) copy-start(u32[32]{0:T(128)} %constant.6) | copy-start | bytes 388
Sparse Core Ops, SparseCore 0:
  9.5 50.2 all-gather.1
  74.9 19.5 all-reduce.2
where the time goes:
time: 104 us; the launch traced here: 103 us
  waiting for transfers between devices  70.9 us (68%)
  between operations  14.1 us (14%)
  matrix products  10.2 us (10%)
  local copies, waits for them, and re-layouts  7.32 us (7%)
    all_gather x1, waiting for transfers between devices, shards(): piece = lax.all_gather(amplitudes, 'ab', axis=1, tiled=True)  51.7 us
    unnamed x3, waiting for transfers between devices  19.2 us
    dot_general x1, matrix products, shards(): lax.dot_general(piece, masked, (((piece.ndim - 1,), (1,)), ((), ())), pre...  10.2 us
    unnamed x6, local copies, waits for them, and re-layouts  4.43 us
  transfers between devices with their start and end apart: 2, of which 2 were waited for; matrix products, arithmetic and copies ran while one was open for 1% of the time, Pallas kernels for 0%

commit v1 on v0

v1 whole, which is shorter than its diff:
```python
import functools

import jax
import jax.numpy as jnp
import numpy as np
from jax import lax
from jax.experimental import pallas as pl
from jax.experimental.pallas import tpu as pltpu
from jax.sharding import PartitionSpec as P

TILE = 128
SLOTS = 16
VMEM_LIMIT = 48 * 2**20


def ring_order(count):
    bits = count.bit_length() - 1
    if count != 1 << bits or bits < 2:
        return list(range(count))
    rows = 1 << ((bits + 1) // 2)
    columns = count // rows
    order = [row * columns for row in range(rows)]
    for at, row in enumerate(reversed(range(rows))):
        across = range(1, columns) if at % 2 == 0 else range(columns - 1, 0, -1)
        order += [row * columns + column for column in across]
    return order


def pick_kernel(ab_tiles, cd_tiles, pattern, ab_irrep, cd_irrep, integrals, listed, high, low, landed, sems):
    def row(p, count):
        label = ab_irrep[p]

        def column(q, count):
            listed[1 + count] = p * cd_tiles + q
            keep = jnp.logical_and(pattern[p, q] == 1, label == cd_irrep[q])
            return count + keep.astype(jnp.int32)

        return lax.fori_loop(0, cd_tiles, column, count, unroll=True)

    count = lax.fori_loop(0, ab_tiles, row, jnp.int32(0))
    listed[0] = count

    def fetch(k):
        tile = listed[1 + k]
        p = tile // cd_tiles
        q = tile - p * cd_tiles
        slot = k % SLOTS
        return pltpu.make_async_copy(
            integrals.at[pl.ds(pl.multiple_of(p * TILE, TILE), TILE), pl.ds(pl.multiple_of(q * TILE, TILE), TILE)],
            landed.at[slot],
            sems.at[slot],
        )

    def begin(k, carry):
        fetch(k).start()
        return carry

    lax.fori_loop(0, jnp.minimum(count, SLOTS), begin, 0)

    def split(k, carry):
        fetch(k).wait()
        tile = landed[k % SLOTS].T
        upper = tile.astype(jnp.bfloat16)
        high[k] = upper
        low[k] = (tile - upper.astype(jnp.float32)).astype(jnp.bfloat16)

        @pl.when(k + SLOTS < count)
        def _():
            fetch(k + SLOTS).start()

        return carry

    lax.fori_loop(0, count, split, 0)


def contract_kernel(spans, rows, half, cd_tiles, listed, places, high, low, *refs):
    pieces, (mine, send, total) = refs[:-3], refs[-3:]
    total[...] = jnp.zeros_like(total)

    def step(k, carry):
        tile = listed[1 + k]
        p = tile // cd_tiles
        q = tile - p * cd_tiles
        columns = pl.ds(pl.multiple_of(q * TILE, TILE), TILE)
        left = jnp.concatenate([piece[0, :, columns] for piece in pieces], axis=0)
        upper = left.astype(jnp.bfloat16)
        lower = (left - upper.astype(jnp.float32)).astype(jnp.bfloat16)
        dot = functools.partial(jnp.dot, preferred_element_type=jnp.float32)
        into = pl.ds(pl.multiple_of(p * TILE, TILE), TILE)
        total[:, into] += dot(upper, high[k]) + (dot(lower, high[k]) + dot(upper, low[k]))
        return carry

    lax.fori_loop(0, listed[0], step, 0)

    for at in range(len(pieces)):
        span = at % spans
        place = places[at // spans]
        block = total[at * rows : (at + 1) * rows, :]

        @pl.when(place < half)
        def _():
            mine[span, pl.ds(pl.multiple_of(place, rows), rows), :] = block

        @pl.when(place >= half)
        def _():
            send[span, pl.ds(pl.multiple_of(place - half, rows), rows), :] = block


def solution(mesh):
    count = mesh.shape["ab"]
    order = ring_order(count)
    ahead = [(order[at], order[(at + 1) % count]) for at in range(count)]
    back = [(to, start) for start, to in ahead]
    offsets = list(range(-(count // 2), (count + 1) // 2))
    place_of = {device: at for at, device in enumerate(order)}
    owners = np.array([[order[(place_of[d] + o) % count] for o in offsets] for d in range(count)], np.int32)

    def shards(amplitudes, integrals, ab_irrep, cd_irrep, block_pattern):
        spans, rows, depth = amplitudes.shape
        slab = integrals.shape[0]
        ab_tiles, cd_tiles = block_pattern.shape
        tiles = ab_tiles * cd_tiles
        half = rows * count // 2

        listed, high, low = pl.pallas_call(
            functools.partial(pick_kernel, ab_tiles, cd_tiles),
            out_shape=(
                jax.ShapeDtypeStruct((tiles + 2,), jnp.int32),
                jax.ShapeDtypeStruct((tiles, TILE, TILE), jnp.bfloat16),
                jax.ShapeDtypeStruct((tiles, TILE, TILE), jnp.bfloat16),
            ),
            in_specs=[pl.BlockSpec(memory_space=pltpu.SMEM)] * 3 + [pl.BlockSpec(memory_space=pl.ANY)],
            out_specs=(
                pl.BlockSpec(memory_space=pltpu.SMEM),
                pl.BlockSpec(memory_space=pltpu.VMEM),
                pl.BlockSpec(memory_space=pltpu.VMEM),
            ),
            scratch_shapes=[pltpu.VMEM((SLOTS, TILE, TILE), jnp.float32), pltpu.SemaphoreType.DMA((SLOTS,))],
            compiler_params=pltpu.CompilerParams(vmem_limit_bytes=VMEM_LIMIT),
            cost_estimate=pl.CostEstimate(flops=0, bytes_accessed=8 << 20, transcendentals=0),
            name="pick",
        )(block_pattern, ab_irrep, cd_irrep, integrals)

        held = {}
        for span in range(spans):
            own = amplitudes[span : span + 1]
            held[span, 0] = own
            long_way = ahead if span % 2 == 0 else back
            for pairs, sign in ((ahead, -1), (back, 1)):
                hops = count // 2 if pairs is long_way else (count - 1) // 2
                piece = own
                for hop in range(1, hops + 1):
                    piece = lax.ppermute(piece, "ab", pairs)
                    at = sign * hop
                    held[span, -(count // 2) if abs(at) == count // 2 and count % 2 == 0 else at] = piece
        pieces = [held[span, offset] for offset in offsets for span in range(spans)]

        owner = jnp.asarray(owners)[lax.axis_index("ab")]
        core = lax.axis_index("cd")
        start = owner * rows
        places = jnp.where(core == 0, start, (start + half) % (2 * half))

        block = jax.ShapeDtypeStruct((spans, half, slab), jnp.float32)
        mine, send = pl.pallas_call(
            functools.partial(contract_kernel, spans, rows, half, cd_tiles),
            out_shape=(block, block),
            in_specs=[pl.BlockSpec(memory_space=pltpu.SMEM)] * 2
            + [pl.BlockSpec(memory_space=pltpu.VMEM)] * (2 + len(pieces)),
            out_specs=(pl.BlockSpec(memory_space=pltpu.VMEM),) * 2,
            scratch_shapes=[pltpu.VMEM((len(pieces) * rows, slab), jnp.float32)],
            compiler_params=pltpu.CompilerParams(vmem_limit_bytes=VMEM_LIMIT),
            name="contract",
        )(listed, places, high, low, *pieces)
        return mine + lax.ppermute(send, "cd", [(0, 1), (1, 0)])

    in_specs = (
        P("groups", "ab", "cd"),
        P(("groups", "ab"), "cd"),
        P(("groups", "ab")),
        P(("groups", "cd")),
        P(("groups", "ab"), "cd"),
    )
    out_specs = P("groups", "cd", "ab")
    return jax.shard_map(shards, mesh=mesh, in_specs=in_specs, out_specs=out_specs, check_vma=False)
```

time: 104 us -> 43 us (0.41)
  waiting for transfers between devices: 70.9 us -> 7.66 us
  starting transfers between devices: 0.04 us -> 17 us
  between operations: 14.1 us -> 0.08 us
  Pallas kernels: 0 us -> 11.5 us
  matrix products: 10.2 us -> 0 us
  local copies, waits for them, and re-layouts: 7.32 us -> 4.97 us
    all_gather x1 -> x0, waiting for transfers between devices: 51.7 us -> none  [shards(): piece = lax.all_gather(amplitudes, 'ab', axis=1, tiled=True)]
    unnamed x3 -> x0, waiting for transfers between devices: 19.2 us -> none
    ppermute x0 -> x15, starting transfers between devices: none -> 17 us  [the longest x14 11.5 us: shards(): piece = lax.ppermute(piece, 'ab', pairs)]
    pallas_call x0 -> x2, Pallas kernels: none -> 11.5 us  [the longest x1 6.27 us: shards(): pl.pallas_call(functools.partial(contract_kernel, spans, rows, half, cd_t...]
    dot_general x1 -> x0, matrix products: 10.2 us -> none  [shards(): lax.dot_general(piece, masked, (((piece.ndim - 1,), (1,)), ((), ())), pre...]
    ppermute x0 -> x15, waiting for transfers between devices: none -> 7.66 us  [the longest x14 6.12 us: shards(): piece = lax.ppermute(piece, 'ab', pairs)]
    dot_general x1 -> x0, local copies, waits for them, and re-layouts: 1.33 us -> none  [shards(): lax.dot_general(piece, masked, (((piece.ndim - 1,), (1,)), ((), ())), pre...]
    unnamed x6 -> x8, local copies, waits for them, and re-layouts: 4.43 us -> 3.98 us
  transfers between devices with their start and end apart: 2 -> 15, of which waited for: 2 -> 6; matrix products, arithmetic and copies ran while one was open for 1% -> 2% of each run, Pallas kernels for 0% -> 12%
where the time goes in v1:
time: 43 us; the launch traced here: 42.8 us
  starting transfers between devices  17 us (40%)
  Pallas kernels  11.5 us (27%)
  waiting for transfers between devices  7.66 us (18%)
  local copies, waits for them, and re-layouts  4.97 us (12%)
  other arithmetic  1.57 us (4%)
    ppermute x14, starting transfers between devices, shards(): piece = lax.ppermute(piece, 'ab', pairs)  11.5 us
    pallas_call x1, Pallas kernels, shards(): pl.pallas_call(functools.partial(contract_kernel, spans, rows, half, cd_t...  6.27 us
    ppermute x14, waiting for transfers between devices, shards(): piece = lax.ppermute(piece, 'ab', pairs)  6.12 us
    ppermute x1, starting transfers between devices, shards(): return mine + lax.ppermute(send, 'cd', [(0, 1), (1, 0)])  5.45 us
    pallas_call x1, Pallas kernels, shards(): pl.pallas_call(functools.partial(pick_kernel, ab_tiles, cd_tiles), out_sh...  5.27 us
    unnamed x8, local copies, waits for them, and re-layouts  3.98 us
    ppermute x1, waiting for transfers between devices, shards(): return mine + lax.ppermute(send, 'cd', [(0, 1), (1, 0)])  1.54 us
    slice x1, local copies, waits for them, and re-layouts, shards(): own = amplitudes[span:span + 1]  0.99 us
  transfers between devices with their start and end apart: 15, of which 6 were waited for; matrix products, arithmetic and copies ran while one was open for 2% of the time, Pallas kernels for 12%

profile of v1, /device:TPU:1, one launch (start us, length us, event | category | flops | bytes accessed | tf_op | source)
XLA Modules:
  0.0 42.8 jit_solution(16690399645019924815)
XLA Ops:
  0.0 1.0 %fusion.1 = (f32[1,16,2048]{2,1,0:T(8,128)S(1)}, f32[1,16,2048]{2,1,0:T(8,128)S(1)}) fusion(f32[2,16,2048]{2,1,0:T(8,128)} %param.6), kind=kLoop, calls=%fused_computation.6 | loop fusion | bytes 524288 | tf_op jit(solution)/shard_map/slice | solution.py:146
  1.0 2.1 %collective-permute-start.4 = (f32[1,16,2048]{2,1,0:T(8,128)S(1)}, f32[1,16,2048]{2,1,0:T(8,128)S(1)}, u32[]{:S(2)}, u32[]{:S(2)}) collective-permute-start(f32[1,16,2048]{2,1,0:T(8,128)S(1)} %get-tuple-element.15.refs_9_), channel_id=1, source_target_pairs={{4,0},{8,4},{12,8},{14,12},{10,14},{6,10},{2,6},{0,2},{5,1},{9,5},... | collective-permute-start | bytes 393224 | tf_op jit(solution)/shard_map/ppermute | solution.py:153
  3.1 0.1 collective-permute-start
  3.2 1.4 %collective-permute-start.8 = (f32[1,16,2048]{2,1,0:T(8,128)S(1)}, f32[1,16,2048]{2,1,0:T(8,128)S(1)}, u32[]{:S(2)}, u32[]{:S(2)}) collective-permute-start(f32[1,16,2048]{2,1,0:T(8,128)S(1)} %get-tuple-element.15.refs_9_), channel_id=1, source_target_pairs={{0,4},{4,8},{8,12},{12,14},{14,10},{10,6},{6,2},{2,0},{1,5},{5,9},... | collective-permute-start | bytes 393224 | tf_op jit(solution)/shard_map/ppermute | solution.py:153
  4.6 0.1 collective-permute-start.11
  4.7 1.7 %collective-permute-done.4.refs_11_ = f32[1,16,2048]{2,1,0:T(8,128)S(1)} collective-permute-done((f32[1,16,2048]{2,1,0:T(8,128)S(1)}, f32[1,16,2048]{2,1,0:T(8,128)S(1)}, u32[]{:S(2)}, u32[]{:S(2)}) %collective-permute-start.4) | collective-permute-done | bytes 131104 | tf_op jit(solution)/shard_map/ppermute | solution.py:153
  6.4 1.1 %collective-permute-start.5 = (f32[1,16,2048]{2,1,0:T(8,128)S(1)}, f32[1,16,2048]{2,1,0:T(8,128)S(1)}, u32[]{:S(2)}, u32[]{:S(2)}) collective-permute-start(f32[1,16,2048]{2,1,0:T(8,128)S(1)} %collective-permute-done.4.refs_11_), channel_id=1, source_target_pairs={{4,0},{8,4},{12,8},{14,12},{10,14},{6,10},{2,6},{0,2},{5,1},{9,5},... | collective-permute-start | bytes 393224 | tf_op jit(solution)/shard_map/ppermute | solution.py:153
  7.5 0.0 collective-permute-done.refs_6_
  7.5 0.4 collective-permute-start.1
  7.9 2.1 %collective-permute-done.8.refs_7_ = f32[1,16,2048]{2,1,0:T(8,128)S(1)} collective-permute-done((f32[1,16,2048]{2,1,0:T(8,128)S(1)}, f32[1,16,2048]{2,1,0:T(8,128)S(1)}, u32[]{:S(2)}, u32[]{:S(2)}) %collective-permute-start.8) | collective-permute-done | bytes 131104 | tf_op jit(solution)/shard_map/ppermute | solution.py:153
  10.0 0.4 %collective-permute-start.9 = (f32[1,16,2048]{2,1,0:T(8,128)S(1)}, f32[1,16,2048]{2,1,0:T(8,128)S(1)}, u32[]{:S(2)}, u32[]{:S(2)}) collective-permute-start(f32[1,16,2048]{2,1,0:T(8,128)S(1)} %collective-permute-done.8.refs_7_), channel_id=1, source_target_pairs={{0,4},{4,8},{8,12},{12,14},{14,10},{10,6},{6,2},{2,0},{1,5},{5,9},... | collective-permute-start | bytes 393224 | tf_op jit(solution)/shard_map/ppermute | solution.py:153
  10.4 0.0 collective-permute-done.11.refs_10_
  10.4 1.0 %collective-permute-start.12 = (f32[1,16,2048]{2,1,0:T(8,128)S(1)}, f32[1,16,2048]{2,1,0:T(8,128)S(1)}, u32[]{:S(2)}, u32[]{:S(2)}) collective-permute-start(f32[1,16,2048]{2,1,0:T(8,128)S(1)} %collective-permute-done.11.refs_10_), channel_id=1, source_target_pairs={{4,0},{8,4},{12,8},{14,12},{10,14},{6,10},{2,6},{0,2},{5,1},{9,5},... | collective-permute-start | bytes 393224 | tf_op jit(solution)/shard_map/ppermute | solution.py:153
  11.4 0.3 collective-permute-done.5.refs_13_
  11.7 1.2 %collective-permute-start.6 = (f32[1,16,2048]{2,1,0:T(8,128)S(1)}, f32[1,16,2048]{2,1,0:T(8,128)S(1)}, u32[]{:S(2)}, u32[]{:S(2)}) collective-permute-start(f32[1,16,2048]{2,1,0:T(8,128)S(1)} %collective-permute-done.5.refs_13_), channel_id=1, source_target_pairs={{4,0},{8,4},{12,8},{14,12},{10,14},{6,10},{2,6},{0,2},{5,1},{9,5},... | collective-permute-start | bytes 393224 | tf_op jit(solution)/shard_map/ppermute | solution.py:153
  12.8 0.0 collective-permute-done.1.refs_4_
  12.8 0.3 collective-permute-start.2
  13.2 1.6 %collective-permute-done.9.refs_5_ = f32[1,16,2048]{2,1,0:T(8,128)S(1)} collective-permute-done((f32[1,16,2048]{2,1,0:T(8,128)S(1)}, f32[1,16,2048]{2,1,0:T(8,128)S(1)}, u32[]{:S(2)}, u32[]{:S(2)}) %collective-permute-start.9) | collective-permute-done | bytes 131104 | tf_op jit(solution)/shard_map/ppermute | solution.py:153
  14.8 0.8 %collective-permute-start.10 = (f32[1,16,2048]{2,1,0:T(8,128)S(1)}, f32[1,16,2048]{2,1,0:T(8,128)S(1)}, u32[]{:S(2)}, u32[]{:S(2)}) collective-permute-start(f32[1,16,2048]{2,1,0:T(8,128)S(1)} %collective-permute-done.9.refs_5_), channel_id=1, source_target_pairs={{0,4},{4,8},{8,12},{12,14},{14,10},{10,6},{6,2},{2,0},{1,5},{5,9},... | collective-permute-start | bytes 393224 | tf_op jit(solution)/shard_map/ppermute | solution.py:153
  15.6 0.0 collective-permute-done.12.refs_12_
  15.6 0.7 %collective-permute-start.13 = (f32[1,16,2048]{2,1,0:T(8,128)S(1)}, f32[1,16,2048]{2,1,0:T(8,128)S(1)}, u32[]{:S(2)}, u32[]{:S(2)}) collective-permute-start(f32[1,16,2048]{2,1,0:T(8,128)S(1)} %collective-permute-done.12.refs_12_), channel_id=1, source_target_pairs={{4,0},{8,4},{12,8},{14,12},{10,14},{6,10},{2,6},{0,2},{5,1},{9,5},... | collective-permute-start | bytes 393224 | tf_op jit(solution)/shard_map/ppermute | solution.py:153
  16.3 0.0 collective-permute-done.6.refs_15_
  16.3 1.3 %collective-permute-start.7 = (f32[1,16,2048]{2,1,0:T(8,128)S(1)}, f32[1,16,2048]{2,1,0:T(8,128)S(1)}, u32[]{:S(2)}, u32[]{:S(2)}) collective-permute-start(f32[1,16,2048]{2,1,0:T(8,128)S(1)} %collective-permute-done.6.refs_15_), channel_id=1, source_target_pairs={{4,0},{8,4},{12,8},{14,12},{10,14},{6,10},{2,6},{0,2},{5,1},{9,5},... | collective-permute-start | bytes 393224 | tf_op jit(solution)/shard_map/ppermute | solution.py:153
  17.6 0.4 collective-permute-done.2.refs_2_
  18.0 0.6 %collective-permute-start.3 = (f32[1,16,2048]{2,1,0:T(8,128)S(1)}, f32[1,16,2048]{2,1,0:T(8,128)S(1)}, u32[]{:S(2)}, u32[]{:S(2)}) collective-permute-start(f32[1,16,2048]{2,1,0:T(8,128)S(1)} %collective-permute-done.2.refs_2_), channel_id=1, source_target_pairs={{0,4},{4,8},{8,12},{12,14},{14,10},{10,6},{6,2},{2,0},{1,5},{5,9},... | collective-permute-start | bytes 393224 | tf_op jit(solution)/shard_map/ppermute | solution.py:153
  18.6 0.0 copy-start.1
  18.6 0.7 %copy-done.1 = s32[8,16]{1,0:T(8,128)S(1)} copy-done((s32[8,16]{1,0:T(8,128)S(1)}, s32[8,16]{1,0:T(8,128)}, u32[]{:S(2)}) %copy-start.1) | copy-done | bytes 536
  19.3 0.0 copy-start.2
  19.3 0.7 %copy-done.2 = s32[8]{0:T(128)S(1)} copy-done((s32[8]{0:T(128)S(1)}, s32[8]{0:T(128)}, u32[]{:S(2)}) %copy-start.2) | copy-done | bytes 56
  20.0 0.0 copy-start.3
  20.0 0.7 %copy-done.3 = s32[16]{0:T(128)S(1)} copy-done((s32[16]{0:T(128)S(1)}, s32[16]{0:T(128)}, u32[]{:S(2)}) %copy-start.3) | copy-done | bytes 88
  20.6 5.3 %pick.1 = (s32[130]{0:T(256)S(1)}, bf16[128,128,128]{2,1,0:T(8,128)(2,1)S(1)}, bf16[128,128,128]{2,1,0:T(8,128)(2,1)}) custom-call(s32[8,16]{1,0:T(8,128)S(1)} %copy-done.1, s32[8]{0:T(128)S(1)} %copy-done.2, s32[16]{0:T(128)S(1)} %copy-done.3, f32[1024,2048]{1,0:T(8,128)} %integrals.1), custom_call_target="tpu_custom_call" | custom-call | bytes 8388608 | tf_op jit(solution)/shard_map/pick/pallas_call | solution.py:125
  25.9 0.0 copy-start
  25.9 2.0 %copy-done = bf16[128,128,128]{2,1,0:T(8,128)(2,1)} copy-done((bf16[128,128,128]{2,1,0:T(8,128)(2,1)}, bf16[128,128,128]{2,1,0:T(8,128)(2,1)S(1)}, u32[]{:S(2)}) %copy-start) | copy-done | bytes 4194328
  27.9 0.7 %broadcast_select_fusion.places = s32[8]{0:T(128)S(1)} fusion(pred[]{:T(512)S(6)} %eq.5, s32[8,8]{1,0:T(8,128)} %constant.32.clone, s32[]{:T(128)S(6)} %select_n.19), kind=kLoop, calls=%fused_computation.3 | loop fusion | flops 112 | bytes 69 | tf_op jit(solution)/shard_map/jit(_where)/select_n | solution.py:161
  28.6 0.0 collective-permute-done.10.refs_3_
  28.6 0.0 collective-permute-done.13.refs_14_
  28.6 0.0 collective-permute-done.7.refs_1_
  28.6 0.0 collective-permute-done.3.refs_0_
  28.6 6.3 %contract.1 = (f32[2,64,1024]{2,1,0:T(8,128)S(1)}, f32[2,64,1024]{2,1,0:T(8,128)S(1)}) custom-call(s32[130]{0:T(256)S(1)} %get-tuple-element.10.listed, s32[8]{0:T(128)S(1)} %broadcast_select_fusion.places, bf16[128,128,128]{2,1,0:T(8,128)(2,1)} %copy-done, bf16[128,128,128]{2,1,0:T(8,128)(2,1)} %get-tuple-element.12.low, ...), custom_call_target="tpu_custom_call" | custom-call | tf_op jit(solution)/shard_map/contract/pallas_call | solution.py:164
  34.9 5.5 %collective-permute-start.14 = (f32[2,64,1024]{2,1,0:T(8,128)S(1)}, f32[2,64,1024]{2,1,0:T(8,128)S(1)}, u32[]{:S(2)}, u32[]{:S(2)}) collective-permute-start(f32[2,64,1024]{2,1,0:T(8,128)S(1)} %get-tuple-element.14), channel_id=1, source_target_pairs={{0,1},{1,0},{2,3},{3,2},{4,5},{5,4},{6,7},{7,6},{8,9},{9,8},{10,11... | collective-permute-start | bytes 1572872 | tf_op jit(solution)/shard_map/ppermute | solution.py:174
  40.4 1.5 %collective-permute-done.14 = f32[2,64,1024]{2,1,0:T(8,128)S(1)} collective-permute-done((f32[2,64,1024]{2,1,0:T(8,128)S(1)}, f32[2,64,1024]{2,1,0:T(8,128)S(1)}, u32[]{:S(2)}, u32[]{:S(2)}) %collective-permute-start.14) | collective-permute-done | bytes 524320 | tf_op jit(solution)/shard_map/ppermute | solution.py:174
  41.9 0.9 %add.18 = f32[2,64,1024]{2,1,0:T(8,128)} add(f32[2,64,1024]{2,1,0:T(8,128)S(1)} %get-tuple-element.13, f32[2,64,1024]{2,1,0:T(8,128)S(1)} %collective-permute-done.14) | non-fusion elementwise | flops 131072 | bytes 1572864 | tf_op jit(solution)/shard_map/add | solution.py:174
Async XLA Ops:
  1.0 5.4 %collective-permute-start.4 = (f32[1,16,2048]{2,1,0:T(8,128)S(1)}, f32[1,16,2048]{2,1,0:T(8,128)S(1)}, u32[]{:S(2)}, u32[]{:S(2)}) collective-permute-start(f32[1,16,2048]{2,1,0:T(8,128)S(1)} %get-tuple-element.15.refs_9_), channel_id=1, source_target_pairs={{4,0},{8,4},{12,8},{14,12},{10,14},{6,10},{2,6},{0,2},{5,1},{9,5},... | collective-permute-start | bytes 393224 | tf_op jit(solution)/shard_map/ppermute | solution.py:153
  3.1 4.4 %collective-permute-start = (f32[1,16,2048]{2,1,0:T(8,128)S(1)}, f32[1,16,2048]{2,1,0:T(8,128)S(1)}, u32[]{:S(2)}, u32[]{:S(2)}) collective-permute-start(f32[1,16,2048]{2,1,0:T(8,128)S(1)} %get-tuple-element.16.refs_8_), channel_id=1, source_target_pairs={{0,4},{4,8},{8,12},{12,14},{14,10},{10,6},{6,2},{2,0},{1,5},{5,9},... | collective-permute-start | bytes 393224 | tf_op jit(solution)/shard_map/ppermute | solution.py:153
  3.2 6.7 %collective-permute-start.8 = (f32[1,16,2048]{2,1,0:T(8,128)S(1)}, f32[1,16,2048]{2,1,0:T(8,128)S(1)}, u32[]{:S(2)}, u32[]{:S(2)}) collective-permute-start(f32[1,16,2048]{2,1,0:T(8,128)S(1)} %get-tuple-element.15.refs_9_), channel_id=1, source_target_pairs={{0,4},{4,8},{8,12},{12,14},{14,10},{10,6},{6,2},{2,0},{1,5},{5,9},... | collective-permute-start | bytes 393224 | tf_op jit(solution)/shard_map/ppermute | solution.py:153
  4.6 5.8 %collective-permute-start.11 = (f32[1,16,2048]{2,1,0:T(8,128)S(1)}, f32[1,16,2048]{2,1,0:T(8,128)S(1)}, u32[]{:S(2)}, u32[]{:S(2)}) collective-permute-start(f32[1,16,2048]{2,1,0:T(8,128)S(1)} %get-tuple-element.16.refs_8_), channel_id=1, source_target_pairs={{4,0},{8,4},{12,8},{14,12},{10,14},{6,10},{2,6},{0,2},{5,1},{9,5},... | collective-permute-start | bytes 393224 | tf_op jit(solution)/shard_map/ppermute | solution.py:153
  6.4 5.3 %collective-permute-start.5 = (f32[1,16,2048]{2,1,0:T(8,128)S(1)}, f32[1,16,2048]{2,1,0:T(8,128)S(1)}, u32[]{:S(2)}, u32[]{:S(2)}) collective-permute-start(f32[1,16,2048]{2,1,0:T(8,128)S(1)} %collective-permute-done.4.refs_11_), channel_id=1, source_target_pairs={{4,0},{8,4},{12,8},{14,12},{10,14},{6,10},{2,6},{0,2},{5,1},{9,5},... | collective-permute-start | bytes 393224 | tf_op jit(solution)/shard_map/ppermute | solution.py:153
  7.5 5.4 %collective-permute-start.1 = (f32[1,16,2048]{2,1,0:T(8,128)S(1)}, f32[1,16,2048]{2,1,0:T(8,128)S(1)}, u32[]{:S(2)}, u32[]{:S(2)}) collective-permute-start(f32[1,16,2048]{2,1,0:T(8,128)S(1)} %collective-permute-done.refs_6_), channel_id=1, source_target_pairs={{0,4},{4,8},{8,12},{12,14},{14,10},{10,6},{6,2},{2,0},{1,5},{5,9},... | collective-permute-start | bytes 393224 | tf_op jit(solution)/shard_map/ppermute | solution.py:153
  10.0 4.8 %collective-permute-start.9 = (f32[1,16,2048]{2,1,0:T(8,128)S(1)}, f32[1,16,2048]{2,1,0:T(8,128)S(1)}, u32[]{:S(2)}, u32[]{:S(2)}) collective-permute-start(f32[1,16,2048]{2,1,0:T(8,128)S(1)} %collective-permute-done.8.refs_7_), channel_id=1, source_target_pairs={{0,4},{4,8},{8,12},{12,14},{14,10},{10,6},{6,2},{2,0},{1,5},{5,9},... | collective-permute-start | bytes 393224 | tf_op jit(solution)/shard_map/ppermute | solution.py:153
  10.4 5.2 %collective-permute-start.12 = (f32[1,16,2048]{2,1,0:T(8,128)S(1)}, f32[1,16,2048]{2,1,0:T(8,128)S(1)}, u32[]{:S(2)}, u32[]{:S(2)}) collective-permute-start(f32[1,16,2048]{2,1,0:T(8,128)S(1)} %collective-permute-done.11.refs_10_), channel_id=1, source_target_pairs={{4,0},{8,4},{12,8},{14,12},{10,14},{6,10},{2,6},{0,2},{5,1},{9,5},... | collective-permute-start | bytes 393224 | tf_op jit(solution)/shard_map/ppermute | solution.py:153
  11.7 4.6 %collective-permute-start.6 = (f32[1,16,2048]{2,1,0:T(8,128)S(1)}, f32[1,16,2048]{2,1,0:T(8,128)S(1)}, u32[]{:S(2)}, u32[]{:S(2)}) collective-permute-start(f32[1,16,2048]{2,1,0:T(8,128)S(1)} %collective-permute-done.5.refs_13_), channel_id=1, source_target_pairs={{4,0},{8,4},{12,8},{14,12},{10,14},{6,10},{2,6},{0,2},{5,1},{9,5},... | collective-permute-start | bytes 393224 | tf_op jit(solution)/shard_map/ppermute | solution.py:153
  12.8 5.1 %collective-permute-start.2 = (f32[1,16,2048]{2,1,0:T(8,128)S(1)}, f32[1,16,2048]{2,1,0:T(8,128)S(1)}, u32[]{:S(2)}, u32[]{:S(2)}) collective-permute-start(f32[1,16,2048]{2,1,0:T(8,128)S(1)} %collective-permute-done.1.refs_4_), channel_id=1, source_target_pairs={{0,4},{4,8},{8,12},{12,14},{14,10},{10,6},{6,2},{2,0},{1,5},{5,9},... | collective-permute-start | bytes 393224 | tf_op jit(solution)/shard_map/ppermute | solution.py:153
  14.8 13.8 %collective-permute-start.10 = (f32[1,16,2048]{2,1,0:T(8,128)S(1)}, f32[1,16,2048]{2,1,0:T(8,128)S(1)}, u32[]{:S(2)}, u32[]{:S(2)}) collective-permute-start(f32[1,16,2048]{2,1,0:T(8,128)S(1)} %collective-permute-done.9.refs_5_), channel_id=1, source_target_pairs={{0,4},{4,8},{8,12},{12,14},{14,10},{10,6},{6,2},{2,0},{1,5},{5,9},... | collective-permute-start | bytes 393224 | tf_op jit(solution)/shard_map/ppermute | solution.py:153
  15.6 13.0 %collective-permute-start.13 = (f32[1,16,2048]{2,1,0:T(8,128)S(1)}, f32[1,16,2048]{2,1,0:T(8,128)S(1)}, u32[]{:S(2)}, u32[]{:S(2)}) collective-permute-start(f32[1,16,2048]{2,1,0:T(8,128)S(1)} %collective-permute-done.12.refs_12_), channel_id=1, source_target_pairs={{4,0},{8,4},{12,8},{14,12},{10,14},{6,10},{2,6},{0,2},{5,1},{9,5},... | collective-permute-start | bytes 393224 | tf_op jit(solution)/shard_map/ppermute | solution.py:153
  16.3 12.3 %collective-permute-start.7 = (f32[1,16,2048]{2,1,0:T(8,128)S(1)}, f32[1,16,2048]{2,1,0:T(8,128)S(1)}, u32[]{:S(2)}, u32[]{:S(2)}) collective-permute-start(f32[1,16,2048]{2,1,0:T(8,128)S(1)} %collective-permute-done.6.refs_15_), channel_id=1, source_target_pairs={{4,0},{8,4},{12,8},{14,12},{10,14},{6,10},{2,6},{0,2},{5,1},{9,5},... | collective-permute-start | bytes 393224 | tf_op jit(solution)/shard_map/ppermute | solution.py:153
  18.0 10.6 %collective-permute-start.3 = (f32[1,16,2048]{2,1,0:T(8,128)S(1)}, f32[1,16,2048]{2,1,0:T(8,128)S(1)}, u32[]{:S(2)}, u32[]{:S(2)}) collective-permute-start(f32[1,16,2048]{2,1,0:T(8,128)S(1)} %collective-permute-done.2.refs_2_), channel_id=1, source_target_pairs={{0,4},{4,8},{8,12},{12,14},{14,10},{10,6},{6,2},{2,0},{1,5},{5,9},... | collective-permute-start | bytes 393224 | tf_op jit(solution)/shard_map/ppermute | solution.py:153
  18.6 0.7 %copy-start.1 = (s32[8,16]{1,0:T(8,128)S(1)}, s32[8,16]{1,0:T(8,128)}, u32[]{:S(2)}) copy-start(s32[8,16]{1,0:T(8,128)} %pattern.1) | copy-start | bytes 1540
  19.3 0.7 %copy-start.2 = (s32[8]{0:T(128)S(1)}, s32[8]{0:T(128)}, u32[]{:S(2)}) copy-start(s32[8]{0:T(128)} %ab_irrep.1) | copy-start | bytes 100
  20.0 0.7 %copy-start.3 = (s32[16]{0:T(128)S(1)}, s32[16]{0:T(128)}, u32[]{:S(2)}) copy-start(s32[16]{0:T(128)} %cd_irrep.1) | copy-start | bytes 196
  25.9 2.0 %copy-start = (bf16[128,128,128]{2,1,0:T(8,128)(2,1)}, bf16[128,128,128]{2,1,0:T(8,128)(2,1)S(1)}, u32[]{:S(2)}) copy-start(bf16[128,128,128]{2,1,0:T(8,128)(2,1)S(1)} %get-tuple-element.11.high) | copy-start | bytes 12582916
  34.9 7.0 %collective-permute-start.14 = (f32[2,64,1024]{2,1,0:T(8,128)S(1)}, f32[2,64,1024]{2,1,0:T(8,128)S(1)}, u32[]{:S(2)}, u32[]{:S(2)}) collective-permute-start(f32[2,64,1024]{2,1,0:T(8,128)S(1)} %get-tuple-element.14), channel_id=1, source_target_pairs={{0,1},{1,0},{2,3},{3,2},{4,5},{5,4},{6,7},{7,6},{8,9},{9,8},{10,11... | collective-permute-start | bytes 1572872 | tf_op jit(solution)/shard_map/ppermute | solution.py:174

commit v2 on v0

v2 whole, which is shorter than its diff:
```python
import functools

import jax
import jax.numpy as jnp
from jax import lax
from jax.experimental import pallas as pl
from jax.experimental.pallas import tpu as pltpu
from jax.sharding import PartitionSpec as P

TILE = 128
UNROLL = 4
FLIGHT = 32
VMEM_LIMIT = 12 * 2**20


def grid_of(count):
    bits = count.bit_length() - 1
    if count != 1 << bits or bits < 2:
        return count, 1
    rows = 1 << ((bits + 1) // 2)
    return rows, count // rows


def at_ring(place, rows, columns):
    if columns == 1:
        return place
    wide = columns - 1
    beyond = place - rows
    line = beyond // wide
    step = beyond - line * wide
    even = (line % 2) == 0
    if isinstance(place, int):
        back = (rows - 1 - line) * columns + (1 + step if even else columns - 1 - step)
        return place * columns if place < rows else back
    back = (rows - 1 - line) * columns + jnp.where(even, 1 + step, columns - 1 - step)
    return jnp.where(place < rows, place * columns, back)


def ring_of(index, rows, columns):
    if columns == 1:
        return index
    wide = columns - 1
    row = index // columns
    column = index - row * columns
    line = rows - 1 - row
    step = jnp.where((line % 2) == 0, column - 1, columns - 1 - column)
    return jnp.where(column == 0, row, rows + line * wide + step)


def pick_kernel(count, offsets, rows, ab_tiles, cd_tiles, pattern, ab_irrep, cd_irrep, integrals, listed, split, landed, sems):
    def row(p, found):
        label = ab_irrep[p]
        for q in range(cd_tiles):
            listed[1 + found] = p * cd_tiles + q
            keep = jnp.logical_and(pattern[p, q] == 1, label == cd_irrep[q])
            found = found + keep.astype(jnp.int32)
        return found

    found = lax.fori_loop(0, ab_tiles, row, jnp.int32(0))
    listed[0] = found

    def fetch(k):
        tile = listed[1 + k]
        p = tile // cd_tiles
        q = tile - p * cd_tiles
        slot = k % FLIGHT
        return pltpu.make_async_copy(
            integrals.at[pl.ds(pl.multiple_of(p * TILE, TILE), TILE), pl.ds(pl.multiple_of(q * TILE, TILE), TILE)],
            landed.at[slot],
            sems.at[slot],
        )

    def begin(k, carry):
        fetch(k).start()
        return carry

    lax.fori_loop(0, jnp.minimum(found, FLIGHT), begin, 0)

    for extra in range(UNROLL):
        listed[1 + found + extra] = 0
        split[found + extra] = jnp.zeros((TILE, 2 * TILE), jnp.bfloat16)
    grid = grid_of(count)
    here = ring_of(lax.axis_index("ab"), *grid)
    first = 1 + ab_tiles * cd_tiles + UNROLL
    half = rows * count // 2
    turn = lax.axis_index("cd") * half
    for at, offset in enumerate(offsets):
        start = at_ring((here + offset + count) % count, *grid) * rows + turn
        listed[first + at] = jnp.where(start >= 2 * half, start - 2 * half, start)

    def part(k, carry):
        fetch(k).wait()
        tile = landed[k % FLIGHT].T
        upper = tile.astype(jnp.bfloat16)
        split[k, :, :TILE] = upper
        split[k, :, TILE:] = (tile - upper.astype(jnp.float32)).astype(jnp.bfloat16)

        @pl.when(k + FLIGHT < found)
        def _():
            fetch(k + FLIGHT).start()

        return carry

    lax.fori_loop(0, found, part, 0)


def products(cd_tiles, listed, split, pieces, total):
    total[...] = jnp.zeros_like(total)

    def step(round_at, carry):
        for unrolled in range(UNROLL):
            k = round_at * UNROLL + unrolled
            tile = listed[1 + k]
            p = tile // cd_tiles
            q = tile - p * cd_tiles
            columns = pl.ds(pl.multiple_of(q * TILE, TILE), TILE)
            left = jnp.concatenate([piece[0, :, columns] for piece in pieces], axis=0)
            upper = left.astype(jnp.bfloat16)
            lower = (left - upper.astype(jnp.float32)).astype(jnp.bfloat16)
            both = jnp.dot(jnp.concatenate([upper, lower], axis=0), split[k], preferred_element_type=jnp.float32)
            high, low = both[: left.shape[0]], both[left.shape[0] :]
            into = pl.ds(pl.multiple_of(p * TILE, TILE), TILE)
            total[:, into] += high[:, :TILE] + (high[:, TILE:] + (low[:, :TILE] + low[:, TILE:]))
        return carry

    lax.fori_loop(0, (listed[0] + UNROLL - 1) // UNROLL, step, 0)


def step_kernel(spans, rows, half, cd_tiles, chunks, listed, split, *refs):
    pieces = refs[: len(chunks) * spans]
    mine, send, total = refs[-3:]
    products(cd_tiles, listed, split, pieces, total)
    for at, chunk in enumerate(chunks):
        place = listed[chunk]
        for span in range(spans):
            from_row = (at * spans + span) * rows
            block = total[from_row : from_row + rows, :]

            @pl.when(place < half)
            def _():
                mine[span, pl.ds(pl.multiple_of(place, rows), rows), :] = block

            @pl.when(place >= half)
            def _():
                send[span, pl.ds(pl.multiple_of(place - half, rows), rows), :] = block


def last_kernel(cd_tiles, listed, split, *refs):
    products(cd_tiles, listed, split, refs[:-1], refs[-1])


def solution(mesh):
    count = mesh.shape["ab"]
    grid = grid_of(count)
    ahead = [(at_ring(at, *grid), at_ring((at + 1) % count, *grid)) for at in range(count)]
    back = [(to, start) for start, to in ahead]
    far = count // 2
    steps = [[0]] + [[-hop, hop] for hop in range(1, far)] + [[-far]]
    offsets = [offset for step in steps for offset in step]

    def shards(amplitudes, integrals, ab_irrep, cd_irrep, block_pattern):
        spans, rows, depth = amplitudes.shape
        slab = integrals.shape[0]
        ab_tiles, cd_tiles = block_pattern.shape
        tiles = ab_tiles * cd_tiles
        half = rows * far
        first = 1 + tiles + UNROLL

        in_hbm = functools.partial(pltpu.with_memory_space_constraint, memory_space=pltpu.HBM)
        smem = pl.BlockSpec(memory_space=pltpu.SMEM)
        vmem = pl.BlockSpec(memory_space=pltpu.VMEM)
        params = pltpu.CompilerParams(vmem_limit_bytes=VMEM_LIMIT)

        listed, split = pl.pallas_call(
            functools.partial(pick_kernel, count, offsets, rows, ab_tiles, cd_tiles),
            out_shape=(
                jax.ShapeDtypeStruct((first + len(offsets),), jnp.int32),
                pltpu.VMEM((tiles + UNROLL, TILE, 2 * TILE), jnp.bfloat16),
            ),
            in_specs=[smem, smem, smem, pl.BlockSpec(memory_space=pltpu.HBM)],
            out_specs=(smem, vmem),
            scratch_shapes=[pltpu.VMEM((FLIGHT, TILE, TILE), jnp.float32), pltpu.SemaphoreType.DMA((FLIGHT,))],
            compiler_params=params,
            cost_estimate=pl.CostEstimate(flops=0, bytes_accessed=8 << 20, transcendentals=0),
            name="pick",
        )(in_hbm(block_pattern), in_hbm(ab_irrep), in_hbm(cd_irrep), in_hbm(integrals))

        held = {}
        for span in range(spans):
            own = amplitudes[span : span + 1]
            held[span, 0] = own
            for pairs, sign in ((ahead, -1), (back, 1)):
                piece = own
                for hop in range(1, far + 1 if (sign < 0) == (span % 2 == 0) else far):
                    piece = lax.ppermute(piece, "ab", pairs)
                    held[span, -far if hop == far else sign * hop] = piece

        block = pltpu.VMEM((spans, half, slab), jnp.float32)
        parts = ()
        for group in [steps[0] + steps[1]] + steps[2:-1]:
            pieces = [held[span, offset] for offset in group for span in range(spans)]
            chunks = [first + offsets.index(offset) for offset in group]
            parts = pl.pallas_call(
                functools.partial(step_kernel, spans, rows, half, cd_tiles, chunks),
                out_shape=(block, block),
                in_specs=[smem] + [vmem] * (1 + len(pieces) + len(parts)),
                out_specs=(vmem, vmem),
                scratch_shapes=[pltpu.VMEM((len(pieces) * rows, slab), jnp.float32)],
                compiler_params=params,
                input_output_aliases={2 + len(pieces): 0, 3 + len(pieces): 1} if parts else {},
                cost_estimate=pl.CostEstimate(flops=1 << 30, bytes_accessed=4 << 20, transcendentals=0),
                name="step",
            )(listed, split, *pieces, *parts)
        mine, send = parts
        swap = [(0, 1), (1, 0)]
        base = mine + lax.ppermute(send, "cd", swap)

        pieces = [held[span, -far] for span in range(spans)]
        last = pl.pallas_call(
            functools.partial(last_kernel, cd_tiles),
            out_shape=pltpu.VMEM((spans * rows, slab), jnp.float32),
            in_specs=[smem] + [vmem] * (1 + len(pieces)),
            out_specs=vmem,
            compiler_params=params,
            cost_estimate=pl.CostEstimate(flops=1 << 34, bytes_accessed=4 << 20, transcendentals=0),
            name="last",
        )(listed, split, *pieces)
        last = last + lax.ppermute(last, "cd", swap)
        place = listed[first + len(offsets) - 1] // rows
        here = (jnp.arange(far, dtype=jnp.int32) == place)[None, :, None, None]
        out = jnp.where(here, last.reshape(spans, 1, rows, slab), base.reshape(spans, far, rows, slab))
        return out.reshape(spans, half, slab)

    in_specs = (
        P("groups", "ab", "cd"),
        P(("groups", "ab"), "cd"),
        P(("groups", "ab")),
        P(("groups", "cd")),
        P(("groups", "ab"), "cd"),
    )
    out_specs = P("groups", "cd", "ab")
    return jax.shard_map(shards, mesh=mesh, in_specs=in_specs, out_specs=out_specs, check_vma=False)
```

time: 104 us -> 38.2 us (0.37)
  waiting for transfers between devices: 70.9 us -> 3.84 us
  starting transfers between devices: 0.04 us -> 18.7 us
  between operations: 14.1 us -> 2.71 us
  Pallas kernels: 0 us -> 10.4 us
  matrix products: 10.2 us -> 0 us
  local copies, waits for them, and re-layouts: 7.32 us -> 1.73 us
    all_gather x1 -> x0, waiting for transfers between devices: 51.7 us -> none  [shards(): piece = lax.all_gather(amplitudes, 'ab', axis=1, tiled=True)]
    unnamed x3 -> x0, waiting for transfers between devices: 19.2 us -> none
    ppermute x0 -> x16, starting transfers between devices: none -> 18.7 us  [the longest x14 11.3 us: shards(): piece = lax.ppermute(piece, 'ab', pairs)]
    pallas_call x0 -> x5, Pallas kernels: none -> 10.4 us  [the longest x3 4.78 us: shards(): pl.pallas_call(functools.partial(step_kernel, spans, rows, half, cd_tiles...]
    dot_general x1 -> x0, matrix products: 10.2 us -> none  [shards(): lax.dot_general(piece, masked, (((piece.ndim - 1,), (1,)), ((), ())), pre...]
    unnamed x6 -> x0, local copies, waits for them, and re-layouts: 4.43 us -> none
    ppermute x0 -> x16, waiting for transfers between devices: none -> 3.84 us  [the longest x14 3.83 us: shards(): piece = lax.ppermute(piece, 'ab', pairs)]
    slice x0 -> x2, local copies, waits for them, and re-layouts: none -> 1.57 us  [the longest x1 0.99 us: shards(): own = amplitudes[span:span + 1]]
  transfers between devices with their start and end apart: 2 -> 16, of which waited for: 2 -> 3; matrix products, arithmetic and copies ran while one was open for 1% -> 2% of each run, Pallas kernels for 0% -> 27%
where the time goes in v2:
time: 38.2 us; the launch traced here: 38.3 us
  starting transfers between devices  18.7 us (49%)
  Pallas kernels  10.4 us (27%)
  waiting for transfers between devices  3.84 us (10%)
  between operations  2.71 us (7%)
  local copies, waits for them, and re-layouts  1.73 us (5%)
  other arithmetic  0.92 us (2%)
    ppermute x14, starting transfers between devices, shards(): piece = lax.ppermute(piece, 'ab', pairs)  11.3 us
    ppermute x1, starting transfers between devices, shards(): base = mine + lax.ppermute(send, 'cd', swap)  5.5 us
    pallas_call x3, Pallas kernels, shards(): pl.pallas_call(functools.partial(step_kernel, spans, rows, half, cd_tiles...  4.78 us
    pallas_call x1, Pallas kernels, shards(): pl.pallas_call(functools.partial(pick_kernel, count, offsets, rows, ab_ti...  4.3 us
    ppermute x14, waiting for transfers between devices, shards(): piece = lax.ppermute(piece, 'ab', pairs)  3.83 us
    ppermute x1, starting transfers between devices, shards(): last = last + lax.ppermute(last, 'cd', swap)  1.86 us
    pallas_call x1, Pallas kernels, shards(): pl.pallas_call(functools.partial(last_kernel, cd_tiles), out_shape=pltpu....  1.31 us
    slice x1, local copies, waits for them, and re-layouts, shards(): own = amplitudes[span:span + 1]  0.99 us
  transfers between devices with their start and end apart: 16, of which 3 were waited for; matrix products, arithmetic and copies ran while one was open for 2% of the time, Pallas kernels for 27%

profile of v2, /device:TPU:1, one launch (start us, length us, event | category | flops | bytes accessed | tf_op | source)
XLA Modules:
  0.0 38.3 jit_solution(2254986407432869747)
XLA Ops:
  0.0 1.0 %fusion = (f32[1,16,2048]{2,1,0:T(8,128)S(1)}, f32[1,16,2048]{2,1,0:T(8,128)S(1)}) fusion(f32[2,16,2048]{2,1,0:T(8,128)} %param.5), kind=kLoop, calls=%fused_computation.2 | loop fusion | bytes 524288 | tf_op jit(solution)/shard_map/slice | solution.py:190
  1.0 2.2 %collective-permute-start = (f32[1,16,2048]{2,1,0:T(8,128)S(1)}, f32[1,16,2048]{2,1,0:T(8,128)S(1)}, u32[]{:S(2)}, u32[]{:S(2)}) collective-permute-start(f32[1,16,2048]{2,1,0:T(8,128)S(1)} %get-tuple-element.22.refs_0_), channel_id=1, source_target_pairs={{0,4},{4,8},{8,12},{12,14},{14,10},{10,6},{6,2},{2,0},{1,5},{5,9},... | collective-permute-start | bytes 393224 | tf_op jit(solution)/shard_map/ppermute | solution.py:195
  3.2 0.0 collective-permute-start.4
  3.2 1.5 %collective-permute-start.9 = (f32[1,16,2048]{2,1,0:T(8,128)S(1)}, f32[1,16,2048]{2,1,0:T(8,128)S(1)}, u32[]{:S(2)}, u32[]{:S(2)}) collective-permute-start(f32[1,16,2048]{2,1,0:T(8,128)S(1)} %get-tuple-element.21.refs_1_), channel_id=1, source_target_pairs={{0,4},{4,8},{8,12},{12,14},{14,10},{10,6},{6,2},{2,0},{1,5},{5,9},... | collective-permute-start | bytes 393224 | tf_op jit(solution)/shard_map/ppermute | solution.py:195
  4.6 0.0 collective-permute-start.12
  4.6 1.7 %collective-permute-done.refs_2_ = f32[1,16,2048]{2,1,0:T(8,128)S(1)} collective-permute-done((f32[1,16,2048]{2,1,0:T(8,128)S(1)}, f32[1,16,2048]{2,1,0:T(8,128)S(1)}, u32[]{:S(2)}, u32[]{:S(2)}) %collective-permute-start) | collective-permute-done | bytes 131104 | tf_op jit(solution)/shard_map/ppermute | solution.py:195
  6.3 1.2 %collective-permute-start.1 = (f32[1,16,2048]{2,1,0:T(8,128)S(1)}, f32[1,16,2048]{2,1,0:T(8,128)S(1)}, u32[]{:S(2)}, u32[]{:S(2)}) collective-permute-start(f32[1,16,2048]{2,1,0:T(8,128)S(1)} %collective-permute-done.refs_2_), channel_id=1, source_target_pairs={{0,4},{4,8},{8,12},{12,14},{14,10},{10,6},{6,2},{2,0},{1,5},{5,9},... | collective-permute-start | bytes 393224 | tf_op jit(solution)/shard_map/ppermute | solution.py:195
  7.5 0.0 collective-permute-done.4.refs_5_
  7.5 0.3 collective-permute-start.5
  7.8 1.3 %collective-permute-done.9.refs_3_ = f32[1,16,2048]{2,1,0:T(8,128)S(1)} collective-permute-done((f32[1,16,2048]{2,1,0:T(8,128)S(1)}, f32[1,16,2048]{2,1,0:T(8,128)S(1)}, u32[]{:S(2)}, u32[]{:S(2)}) %collective-permute-start.9) | collective-permute-done | bytes 131104 | tf_op jit(solution)/shard_map/ppermute | solution.py:195
  9.1 1.2 %collective-permute-start.10 = (f32[1,16,2048]{2,1,0:T(8,128)S(1)}, f32[1,16,2048]{2,1,0:T(8,128)S(1)}, u32[]{:S(2)}, u32[]{:S(2)}) collective-permute-start(f32[1,16,2048]{2,1,0:T(8,128)S(1)} %collective-permute-done.9.refs_3_), channel_id=1, source_target_pairs={{0,4},{4,8},{8,12},{12,14},{14,10},{10,6},{6,2},{2,0},{1,5},{5,9},... | collective-permute-start | bytes 393224 | tf_op jit(solution)/shard_map/ppermute | solution.py:195
  10.3 0.0 collective-permute-done.12.refs_4_
  10.3 0.3 collective-permute-start.13
  10.6 0.8 %collective-permute-done.1.refs_0_ = f32[1,16,2048]{2,1,0:T(8,128)S(1)} collective-permute-done((f32[1,16,2048]{2,1,0:T(8,128)S(1)}, f32[1,16,2048]{2,1,0:T(8,128)S(1)}, u32[]{:S(2)}, u32[]{:S(2)}) %collective-permute-start.1) | collective-permute-done | bytes 131104 | tf_op jit(solution)/shard_map/ppermute | solution.py:195
  11.4 1.5 %collective-permute-start.2 = (f32[1,16,2048]{2,1,0:T(8,128)S(1)}, f32[1,16,2048]{2,1,0:T(8,128)S(1)}, u32[]{:S(2)}, u32[]{:S(2)}) collective-permute-start(f32[1,16,2048]{2,1,0:T(8,128)S(1)} %collective-permute-done.1.refs_0_), channel_id=1, source_target_pairs={{0,4},{4,8},{8,12},{12,14},{14,10},{10,6},{6,2},{2,0},{1,5},{5,9},... | collective-permute-start | bytes 393224 | tf_op jit(solution)/shard_map/ppermute | solution.py:195
  12.9 0.0 collective-permute-done.5.refs_3_
  12.9 0.0 collective-permute-start.6
  12.9 4.3 %pick.1 = (s32[141]{0:T(256)S(1)}, bf16[132,128,256]{2,1,0:T(8,128)(2,1)S(1)}) custom-call(s32[8,16]{1,0:T(8,128)} %pattern.1, s32[8]{0:T(128)} %ab_irrep.1, s32[16]{0:T(128)} %cd_irrep.1, f32[1024,2048]{1,0:T(8,128)} %integrals.1), custom_call_target="tpu_custom_call" | custom-call | bytes 8388608 | tf_op jit(solution)/shard_map/pick/pallas_call | solution.py:174
  17.2 0.0 collective-permute-done.10.refs_1_
  17.2 1.0 %collective-permute-start.11 = (f32[1,16,2048]{2,1,0:T(8,128)S(1)}, f32[1,16,2048]{2,1,0:T(8,128)S(1)}, u32[]{:S(2)}, u32[]{:S(2)}) collective-permute-start(f32[1,16,2048]{2,1,0:T(8,128)S(1)} %collective-permute-done.10.refs_1_), channel_id=1, source_target_pairs={{0,4},{4,8},{8,12},{12,14},{14,10},{10,6},{6,2},{2,0},{1,5},{5,9},... | collective-permute-start | bytes 393224 | tf_op jit(solution)/shard_map/ppermute | solution.py:195
  18.2 0.0 collective-permute-done.13.refs_2_
  18.2 0.5 %collective-permute-start.14 = (f32[1,16,2048]{2,1,0:T(8,128)S(1)}, f32[1,16,2048]{2,1,0:T(8,128)S(1)}, u32[]{:S(2)}, u32[]{:S(2)}) collective-permute-start(f32[1,16,2048]{2,1,0:T(8,128)S(1)} %collective-permute-done.13.refs_2_), channel_id=1, source_target_pairs={{4,0},{8,4},{12,8},{14,12},{10,14},{6,10},{2,6},{0,2},{5,1},{9,5},... | collective-permute-start | bytes 393224 | tf_op jit(solution)/shard_map/ppermute | solution.py:195
  18.8 1.7 %step.3 = (f32[2,64,1024]{2,1,0:T(8,128)S(1)}, f32[2,64,1024]{2,1,0:T(8,128)S(1)}) custom-call(s32[141]{0:T(256)S(1)} %get-tuple-element.13.listed, bf16[132,128,256]{2,1,0:T(8,128)(2,1)S(1)} %get-tuple-element.14.split, f32[1,16,2048]{2,1,0:T(8,128)S(1)} %get-tuple-element.22.refs_0_, f32[1,16,2048]{2,1,0:T(8,128)S(1)} %get-tuple-element.21.refs_1_, ...), custom_call_target="tpu_custom_call" | custom-call | flops 1073741824 | bytes 4194304 | tf_op jit(solution)/shard_map/step/pallas_call | solution.py:203
  20.5 0.0 collective-permute-done.2.refs_0_
  20.5 0.4 %collective-permute-start.3 = (f32[1,16,2048]{2,1,0:T(8,128)S(1)}, f32[1,16,2048]{2,1,0:T(8,128)S(1)}, u32[]{:S(2)}, u32[]{:S(2)}) collective-permute-start(f32[1,16,2048]{2,1,0:T(8,128)S(1)} %collective-permute-done.2.refs_0_), channel_id=1, source_target_pairs={{0,4},{4,8},{8,12},{12,14},{14,10},{10,6},{6,2},{2,0},{1,5},{5,9},... | collective-permute-start | bytes 393224 | tf_op jit(solution)/shard_map/ppermute | solution.py:195
  20.9 0.0 collective-permute-done.6.refs_3_
  21.0 1.3 %collective-permute-start.7 = (f32[1,16,2048]{2,1,0:T(8,128)S(1)}, f32[1,16,2048]{2,1,0:T(8,128)S(1)}, u32[]{:S(2)}, u32[]{:S(2)}) collective-permute-start(f32[1,16,2048]{2,1,0:T(8,128)S(1)} %collective-permute-done.6.refs_3_), channel_id=1, source_target_pairs={{4,0},{8,4},{12,8},{14,12},{10,14},{6,10},{2,6},{0,2},{5,1},{9,5},... | collective-permute-start | bytes 393224 | tf_op jit(solution)/shard_map/ppermute | solution.py:195
  22.2 1.5 %step.4 = (f32[2,64,1024]{2,1,0:T(8,128)S(1)}, f32[2,64,1024]{2,1,0:T(8,128)S(1)}) custom-call(s32[141]{0:T(256)S(1)} %get-tuple-element.13.listed, bf16[132,128,256]{2,1,0:T(8,128)(2,1)S(1)} %get-tuple-element.14.split, f32[1,16,2048]{2,1,0:T(8,128)S(1)} %collective-permute-done.1.refs_0_, ...), custom_call_target="tpu_custom_call", output_to_operand_aliasing={{0}: (6, {}), {1}: (7, {})} | custom-call | flops 1073741824 | bytes 4194304 | tf_op jit(solution)/shard_map/step/pallas_call | solution.py:203
  23.8 0.0 collective-permute-done.11.refs_1_
  23.8 0.0 collective-permute-done.14.refs_2_
  23.8 1.5 %step.5 = (f32[2,64,1024]{2,1,0:T(8,128)S(1)}, f32[2,64,1024]{2,1,0:T(8,128)S(1)}) custom-call(s32[141]{0:T(256)S(1)} %get-tuple-element.13.listed, bf16[132,128,256]{2,1,0:T(8,128)(2,1)S(1)} %get-tuple-element.14.split, f32[1,16,2048]{2,1,0:T(8,128)S(1)} %collective-permute-done.2.refs_0_, ...), custom_call_target="tpu_custom_call", output_to_operand_aliasing={{0}: (6, {}), {1}: (7, {})} | custom-call | flops 1073741824 | bytes 4194304 | tf_op jit(solution)/shard_map/step/pallas_call | solution.py:203
  25.3 5.5 %collective-permute-start.15 = (f32[2,64,1024]{2,1,0:T(8,128)S(1)}, f32[2,64,1024]{2,1,0:T(8,128)S(1)}, u32[]{:S(2)}, u32[]{:S(2)}) collective-permute-start(f32[2,64,1024]{2,1,0:T(8,128)S(1)} %get-tuple-element.20), channel_id=1, source_target_pairs={{0,1},{1,0},{2,3},{3,2},{4,5},{5,4},{6,7},{7,6},{8,9},{9,8},{10,11... | collective-permute-start | bytes 1572872 | tf_op jit(solution)/shard_map/ppermute | solution.py:216
  30.8 0.0 collective-permute-done.3.refs_0_
  30.8 0.0 collective-permute-done.7.refs_1_
  30.8 1.3 %last.1 = f32[32,1024]{1,0:T(8,128)S(1)} custom-call(s32[141]{0:T(256)S(1)} %get-tuple-element.13.listed, bf16[132,128,256]{2,1,0:T(8,128)(2,1)S(1)} %get-tuple-element.14.split, f32[1,16,2048]{2,1,0:T(8,128)S(1)} %collective-permute-done.3.refs_0_, f32[1,16,2048]{2,1,0:T(8,128)S(1)} %collective-permute-done.7.refs_1_), custom_call_target="tpu_custom_call" | custom-call | flops 17179869184 | bytes 4194304 | tf_op jit(solution)/shard_map/last/pallas_call | solution.py:219
  32.1 1.9 %collective-permute-start.8 = (f32[32,1024]{1,0:T(8,128)S(1)}, f32[32,1024]{1,0:T(8,128)S(1)}, u32[]{:S(2)}, u32[]{:S(2)}) collective-permute-start(f32[32,1024]{1,0:T(8,128)S(1)} %last.1), channel_id=1, source_target_pairs={{0,1},{1,0},{2,3},{3,2},{4,5},{5,4},{6,7},{7,6},{8,9},{9,8},{10,11... | collective-permute-start | bytes 393224 | tf_op jit(solution)/shard_map/ppermute | solution.py:228
  34.0 0.6 %slice.9 = s32[1]{0:T(128)} slice(s32[141]{0:T(256)S(1)} %get-tuple-element.13.listed), slice={[140:141]} | slice | bytes 8 | tf_op jit(solution)/shard_map/slice | solution.py:229
  37.2 0.1 broadcast_in_dim.25
  37.3 0.1 broadcast_in_dim.26
  37.4 0.0 collective-permute-done.8
  37.4 0.0 collective-permute-done.15
  37.4 0.9 %bitcast_select_fusion = f32[2,64,1024]{2,1,0:T(8,128)} fusion(f32[2,64,1024]{2,1,0:T(8,128)S(1)} %get-tuple-element.19, f32[2,64,1024]{2,1,0:T(8,128)S(1)} %collective-permute-done.15, f32[2,16,1024]{2,1,0:T(8,128)S(1)} %bitcast.4, pred[64]{0:T(512)(128)(4,1)S(1)} %broadcast_in_dim.26), kind=kLoop, calls=%fused_computation | loop fusion | flops 262144 | bytes 1704000 | tf_op jit(solution)/shard_map/jit(_where)/select_n | solution.py:231
  (2 shorter events, 0.0 us)
Async XLA Ops:
  1.0 5.3 %collective-permute-start = (f32[1,16,2048]{2,1,0:T(8,128)S(1)}, f32[1,16,2048]{2,1,0:T(8,128)S(1)}, u32[]{:S(2)}, u32[]{:S(2)}) collective-permute-start(f32[1,16,2048]{2,1,0:T(8,128)S(1)} %get-tuple-element.22.refs_0_), channel_id=1, source_target_pairs={{0,4},{4,8},{8,12},{12,14},{14,10},{10,6},{6,2},{2,0},{1,5},{5,9},... | collective-permute-start | bytes 393224 | tf_op jit(solution)/shard_map/ppermute | solution.py:195
  3.2 4.4 %collective-permute-start.4 = (f32[1,16,2048]{2,1,0:T(8,128)S(1)}, f32[1,16,2048]{2,1,0:T(8,128)S(1)}, u32[]{:S(2)}, u32[]{:S(2)}) collective-permute-start(f32[1,16,2048]{2,1,0:T(8,128)S(1)} %get-tuple-element.21.refs_1_), channel_id=1, source_target_pairs={{4,0},{8,4},{12,8},{14,12},{10,14},{6,10},{2,6},{0,2},{5,1},{9,5},... | collective-permute-start | bytes 393224 | tf_op jit(solution)/shard_map/ppermute | solution.py:195
  3.2 6.0 %collective-permute-start.9 = (f32[1,16,2048]{2,1,0:T(8,128)S(1)}, f32[1,16,2048]{2,1,0:T(8,128)S(1)}, u32[]{:S(2)}, u32[]{:S(2)}) collective-permute-start(f32[1,16,2048]{2,1,0:T(8,128)S(1)} %get-tuple-element.21.refs_1_), channel_id=1, source_target_pairs={{0,4},{4,8},{8,12},{12,14},{14,10},{10,6},{6,2},{2,0},{1,5},{5,9},... | collective-permute-start | bytes 393224 | tf_op jit(solution)/shard_map/ppermute | solution.py:195
  4.6 5.7 %collective-permute-start.12 = (f32[1,16,2048]{2,1,0:T(8,128)S(1)}, f32[1,16,2048]{2,1,0:T(8,128)S(1)}, u32[]{:S(2)}, u32[]{:S(2)}) collective-permute-start(f32[1,16,2048]{2,1,0:T(8,128)S(1)} %get-tuple-element.22.refs_0_), channel_id=1, source_target_pairs={{4,0},{8,4},{12,8},{14,12},{10,14},{6,10},{2,6},{0,2},{5,1},{9,5},... | collective-permute-start | bytes 393224 | tf_op jit(solution)/shard_map/ppermute | solution.py:195
  6.3 5.0 %collective-permute-start.1 = (f32[1,16,2048]{2,1,0:T(8,128)S(1)}, f32[1,16,2048]{2,1,0:T(8,128)S(1)}, u32[]{:S(2)}, u32[]{:S(2)}) collective-permute-start(f32[1,16,2048]{2,1,0:T(8,128)S(1)} %collective-permute-done.refs_2_), channel_id=1, source_target_pairs={{0,4},{4,8},{8,12},{12,14},{14,10},{10,6},{6,2},{2,0},{1,5},{5,9},... | collective-permute-start | bytes 393224 | tf_op jit(solution)/shard_map/ppermute | solution.py:195
  7.5 5.4 %collective-permute-start.5 = (f32[1,16,2048]{2,1,0:T(8,128)S(1)}, f32[1,16,2048]{2,1,0:T(8,128)S(1)}, u32[]{:S(2)}, u32[]{:S(2)}) collective-permute-start(f32[1,16,2048]{2,1,0:T(8,128)S(1)} %collective-permute-done.4.refs_5_), channel_id=1, source_target_pairs={{4,0},{8,4},{12,8},{14,12},{10,14},{6,10},{2,6},{0,2},{5,1},{9,5},... | collective-permute-start | bytes 393224 | tf_op jit(solution)/shard_map/ppermute | solution.py:195
  9.1 8.1 %collective-permute-start.10 = (f32[1,16,2048]{2,1,0:T(8,128)S(1)}, f32[1,16,2048]{2,1,0:T(8,128)S(1)}, u32[]{:S(2)}, u32[]{:S(2)}) collective-permute-start(f32[1,16,2048]{2,1,0:T(8,128)S(1)} %collective-permute-done.9.refs_3_), channel_id=1, source_target_pairs={{0,4},{4,8},{8,12},{12,14},{14,10},{10,6},{6,2},{2,0},{1,5},{5,9},... | collective-permute-start | bytes 393224 | tf_op jit(solution)/shard_map/ppermute | solution.py:195
  10.3 7.9 %collective-permute-start.13 = (f32[1,16,2048]{2,1,0:T(8,128)S(1)}, f32[1,16,2048]{2,1,0:T(8,128)S(1)}, u32[]{:S(2)}, u32[]{:S(2)}) collective-permute-start(f32[1,16,2048]{2,1,0:T(8,128)S(1)} %collective-permute-done.12.refs_4_), channel_id=1, source_target_pairs={{4,0},{8,4},{12,8},{14,12},{10,14},{6,10},{2,6},{0,2},{5,1},{9,5},... | collective-permute-start | bytes 393224 | tf_op jit(solution)/shard_map/ppermute | solution.py:195
  11.4 9.1 %collective-permute-start.2 = (f32[1,16,2048]{2,1,0:T(8,128)S(1)}, f32[1,16,2048]{2,1,0:T(8,128)S(1)}, u32[]{:S(2)}, u32[]{:S(2)}) collective-permute-start(f32[1,16,2048]{2,1,0:T(8,128)S(1)} %collective-permute-done.1.refs_0_), channel_id=1, source_target_pairs={{0,4},{4,8},{8,12},{12,14},{14,10},{10,6},{6,2},{2,0},{1,5},{5,9},... | collective-permute-start | bytes 393224 | tf_op jit(solution)/shard_map/ppermute | solution.py:195
  12.9 8.0 %collective-permute-start.6 = (f32[1,16,2048]{2,1,0:T(8,128)S(1)}, f32[1,16,2048]{2,1,0:T(8,128)S(1)}, u32[]{:S(2)}, u32[]{:S(2)}) collective-permute-start(f32[1,16,2048]{2,1,0:T(8,128)S(1)} %collective-permute-done.5.refs_3_), channel_id=1, source_target_pairs={{4,0},{8,4},{12,8},{14,12},{10,14},{6,10},{2,6},{0,2},{5,1},{9,5},... | collective-permute-start | bytes 393224 | tf_op jit(solution)/shard_map/ppermute | solution.py:195
  17.2 6.5 %collective-permute-start.11 = (f32[1,16,2048]{2,1,0:T(8,128)S(1)}, f32[1,16,2048]{2,1,0:T(8,128)S(1)}, u32[]{:S(2)}, u32[]{:S(2)}) collective-permute-start(f32[1,16,2048]{2,1,0:T(8,128)S(1)} %collective-permute-done.10.refs_1_), channel_id=1, source_target_pairs={{0,4},{4,8},{8,12},{12,14},{14,10},{10,6},{6,2},{2,0},{1,5},{5,9},... | collective-permute-start | bytes 393224 | tf_op jit(solution)/shard_map/ppermute | solution.py:195
  18.2 5.5 %collective-permute-start.14 = (f32[1,16,2048]{2,1,0:T(8,128)S(1)}, f32[1,16,2048]{2,1,0:T(8,128)S(1)}, u32[]{:S(2)}, u32[]{:S(2)}) collective-permute-start(f32[1,16,2048]{2,1,0:T(8,128)S(1)} %collective-permute-done.13.refs_2_), channel_id=1, source_target_pairs={{4,0},{8,4},{12,8},{14,12},{10,14},{6,10},{2,6},{0,2},{5,1},{9,5},... | collective-permute-start | bytes 393224 | tf_op jit(solution)/shard_map/ppermute | solution.py:195
  20.5 10.3 %collective-permute-start.3 = (f32[1,16,2048]{2,1,0:T(8,128)S(1)}, f32[1,16,2048]{2,1,0:T(8,128)S(1)}, u32[]{:S(2)}, u32[]{:S(2)}) collective-permute-start(f32[1,16,2048]{2,1,0:T(8,128)S(1)} %collective-permute-done.2.refs_0_), channel_id=1, source_target_pairs={{0,4},{4,8},{8,12},{12,14},{14,10},{10,6},{6,2},{2,0},{1,5},{5,9},... | collective-permute-start | bytes 393224 | tf_op jit(solution)/shard_map/ppermute | solution.py:195
  21.0 9.9 %collective-permute-start.7 = (f32[1,16,2048]{2,1,0:T(8,128)S(1)}, f32[1,16,2048]{2,1,0:T(8,128)S(1)}, u32[]{:S(2)}, u32[]{:S(2)}) collective-permute-start(f32[1,16,2048]{2,1,0:T(8,128)S(1)} %collective-permute-done.6.refs_3_), channel_id=1, source_target_pairs={{4,0},{8,4},{12,8},{14,12},{10,14},{6,10},{2,6},{0,2},{5,1},{9,5},... | collective-permute-start | bytes 393224 | tf_op jit(solution)/shard_map/ppermute | solution.py:195
  25.3 12.1 %collective-permute-start.15 = (f32[2,64,1024]{2,1,0:T(8,128)S(1)}, f32[2,64,1024]{2,1,0:T(8,128)S(1)}, u32[]{:S(2)}, u32[]{:S(2)}) collective-permute-start(f32[2,64,1024]{2,1,0:T(8,128)S(1)} %get-tuple-element.20), channel_id=1, source_target_pairs={{0,1},{1,0},{2,3},{3,2},{4,5},{5,4},{6,7},{7,6},{8,9},{9,8},{10,11... | collective-permute-start | bytes 1572872 | tf_op jit(solution)/shard_map/ppermute | solution.py:216
  32.1 5.2 %collective-permute-start.8 = (f32[32,1024]{1,0:T(8,128)S(1)}, f32[32,1024]{1,0:T(8,128)S(1)}, u32[]{:S(2)}, u32[]{:S(2)}) collective-permute-start(f32[32,1024]{1,0:T(8,128)S(1)} %last.1), channel_id=1, source_target_pairs={{0,1},{1,0},{2,3},{3,2},{4,5},{5,4},{6,7},{7,6},{8,9},{9,8},{10,11... | collective-permute-start | bytes 393224 | tf_op jit(solution)/shard_map/ppermute | solution.py:228

commit v3 on v2

v3 whole, which is shorter than its diff:
```python
import functools

import jax
import jax.numpy as jnp
from jax import lax
from jax.experimental import pallas as pl
from jax.experimental.pallas import tpu as pltpu
from jax.sharding import PartitionSpec as P

TILE = 128
UNROLL = 4
FLIGHT = 32
VMEM_LIMIT = 12 * 2**20


def grid_of(count):
    bits = count.bit_length() - 1
    if count != 1 << bits or bits < 2:
        return count, 1
    rows = 1 << ((bits + 1) // 2)
    return rows, count // rows


def at_ring(place, rows, columns):
    if columns == 1:
        return place
    wide = columns - 1
    beyond = place - rows
    line = beyond // wide
    step = beyond - line * wide
    even = (line % 2) == 0
    if isinstance(place, int):
        back = (rows - 1 - line) * columns + (1 + step if even else columns - 1 - step)
        return place * columns if place < rows else back
    back = (rows - 1 - line) * columns + jnp.where(even, 1 + step, columns - 1 - step)
    return jnp.where(place < rows, place * columns, back)


def ring_of(index, rows, columns):
    if columns == 1:
        return index
    wide = columns - 1
    row = index // columns
    column = index - row * columns
    line = rows - 1 - row
    step = jnp.where((line % 2) == 0, column - 1, columns - 1 - column)
    return jnp.where(column == 0, row, rows + line * wide + step)


def places(count, rows, chunks):
    grid = grid_of(count)
    here = ring_of(lax.axis_index("ab"), *grid)
    core = lax.axis_index("cd")
    whole = rows * count
    found = []
    for chain, hop in chunks:
        away = (2 * core - 1) * hop if chain == 0 else (1 - 2 * core) * hop
        start = at_ring((here + away + count) % count, *grid) * rows + core * (whole // 2)
        found.append(jnp.where(start >= whole, start - whole, start))
    return found


def pick_kernel(ab_tiles, cd_tiles, pattern, ab_irrep, cd_irrep, integrals, amplitudes, listed, split, own, landed, sems, own_sem):
    copy = pltpu.make_async_copy(amplitudes, own, own_sem)
    copy.start()

    def fetch(k):
        tile = listed[1 + k]
        p = tile // cd_tiles
        q = tile - p * cd_tiles
        slot = k % FLIGHT
        return pltpu.make_async_copy(
            integrals.at[pl.ds(pl.multiple_of(p * TILE, TILE), TILE), pl.ds(pl.multiple_of(q * TILE, TILE), TILE)],
            landed.at[slot],
            sems.at[slot],
        )

    def begin(k, carry):
        fetch(k).start()
        return carry

    def row(p, found):
        label = ab_irrep[p]
        before = found
        for q in range(cd_tiles):
            listed[1 + found] = p * cd_tiles + q
            keep = jnp.logical_and(pattern[p, q] == 1, label == cd_irrep[q])
            found = found + keep.astype(jnp.int32)
        lax.fori_loop(jnp.minimum(before, FLIGHT), jnp.minimum(found, FLIGHT), begin, 0)
        return found

    found = lax.fori_loop(0, ab_tiles, row, jnp.int32(0))
    listed[0] = found
    for extra in range(UNROLL):
        listed[1 + found + extra] = 0
        split[found + extra] = jnp.zeros((TILE, 2 * TILE), jnp.bfloat16)

    def part(k, carry):
        fetch(k).wait()
        tile = landed[k % FLIGHT].T
        upper = tile.astype(jnp.bfloat16)
        split[k, :, :TILE] = upper
        split[k, :, TILE:] = (tile - upper.astype(jnp.float32)).astype(jnp.bfloat16)

        @pl.when(k + FLIGHT < found)
        def _():
            fetch(k + FLIGHT).start()

        return carry

    lax.fori_loop(0, found, part, 0)
    copy.wait()


def products(cd_tiles, listed, split, pieces, total):
    total[...] = jnp.zeros_like(total)

    def step(round_at, carry):
        for unrolled in range(UNROLL):
            k = round_at * UNROLL + unrolled
            tile = listed[1 + k]
            p = tile // cd_tiles
            q = tile - p * cd_tiles
            columns = pl.ds(pl.multiple_of(q * TILE, TILE), TILE)
            left = jnp.concatenate([piece[span, :, columns] for piece in pieces for span in range(piece.shape[0])], axis=0)
            upper = left.astype(jnp.bfloat16)
            lower = (left - upper.astype(jnp.float32)).astype(jnp.bfloat16)
            both = jnp.dot(jnp.concatenate([upper, lower], axis=0), split[k], preferred_element_type=jnp.float32)
            high, low = both[: left.shape[0]], both[left.shape[0] :]
            into = pl.ds(pl.multiple_of(p * TILE, TILE), TILE)
            total[:, into] += high[:, :TILE] + (high[:, TILE:] + (low[:, :TILE] + low[:, TILE:]))
        return carry

    lax.fori_loop(0, (listed[0] + UNROLL - 1) // UNROLL, step, 0)


def step_kernel(count, spans, rows, cd_tiles, chunks, listed, split, *refs):
    pieces = refs[: len(chunks)]
    mine, send, total = refs[-3:]
    products(cd_tiles, listed, split, pieces, total)
    half = rows * count // 2
    for at, place in enumerate(places(count, rows, chunks)):
        for span in range(spans):
            from_row = (at * spans + span) * rows
            block = total[from_row : from_row + rows, :]

            @pl.when(place < half)
            def _():
                mine[span, pl.ds(pl.multiple_of(place, rows), rows), :] = block

            @pl.when(place >= half)
            def _():
                send[span, pl.ds(pl.multiple_of(place - half, rows), rows), :] = block


def last_kernel(cd_tiles, listed, split, piece, total):
    products(cd_tiles, listed, split, [piece], total)


def merge_kernel(mine, received, out):
    out[...] = mine[...] + received[...]


def final_kernel(count, spans, rows, last, received, before, out, total, sems):
    del before
    (place,) = places(count, rows, [(0, count // 2)])

    @pl.when(place < rows * count // 2)
    def _():
        total[...] = last[...] + received[...]
        copies = []
        for span in range(spans):
            copies.append(
                pltpu.make_async_copy(
                    total.at[pl.ds(span * rows, rows), :],
                    out.at[span, pl.ds(pl.multiple_of(place, rows), rows), :],
                    sems.at[span],
                )
            )
            copies[-1].start()
        for copy in copies:
            copy.wait()


def solution(mesh):
    count = mesh.shape["ab"]
    cores = mesh.shape["cd"]
    grid = grid_of(count)
    far = count // 2
    around = []
    for chain in range(2):
        pairs = []
        for at in range(count):
            for core in range(cores):
                to = at + 1 if core == chain else at + count - 1
                pairs.append((at_ring(at, *grid) * cores + core, at_ring(to % count, *grid) * cores + core))
        around.append(pairs)
    swap = [(0, 1), (1, 0)]

    def shards(amplitudes, integrals, ab_irrep, cd_irrep, block_pattern):
        spans, rows, depth = amplitudes.shape
        slab = integrals.shape[0]
        ab_tiles, cd_tiles = block_pattern.shape
        tiles = ab_tiles * cd_tiles
        half = rows * far

        in_hbm = functools.partial(pltpu.with_memory_space_constraint, memory_space=pltpu.HBM)
        smem = pl.BlockSpec(memory_space=pltpu.SMEM)
        vmem = pl.BlockSpec(memory_space=pltpu.VMEM)
        hbm = pl.BlockSpec(memory_space=pltpu.HBM)
        params = pltpu.CompilerParams(vmem_limit_bytes=VMEM_LIMIT)

        listed, split, own = pl.pallas_call(
            functools.partial(pick_kernel, ab_tiles, cd_tiles),
            out_shape=(
                jax.ShapeDtypeStruct((1 + tiles + UNROLL,), jnp.int32),
                pltpu.VMEM((tiles + UNROLL, TILE, 2 * TILE), jnp.bfloat16),
                pltpu.VMEM(amplitudes.shape, jnp.float32),
            ),
            in_specs=[smem, smem, smem, hbm, hbm],
            out_specs=(smem, vmem, vmem),
            scratch_shapes=[
                pltpu.VMEM((FLIGHT, TILE, TILE), jnp.float32),
                pltpu.SemaphoreType.DMA((FLIGHT,)),
                pltpu.SemaphoreType.DMA,
            ],
            compiler_params=params,
            cost_estimate=pl.CostEstimate(flops=0, bytes_accessed=8 << 20, transcendentals=0),
            name="pick",
        )(in_hbm(block_pattern), in_hbm(ab_irrep), in_hbm(cd_irrep), in_hbm(integrals), in_hbm(amplitudes))

        held = {(0, 0): own}
        for chain, piece, hops in ((0, amplitudes, far), (1, own, far - 1)):
            for hop in range(1, hops + 1):
                piece = lax.ppermute(piece, ("ab", "cd"), around[chain])
                held[chain, hop] = piece

        block = pltpu.VMEM((spans, half, slab), jnp.float32)
        parts = ()
        for group in [[(0, 0), (0, 1)]] + [[(1, hop - 1), (0, hop)] for hop in range(2, far)] + [[(1, far - 1)]]:
            pieces = [held[chunk] for chunk in group]
            parts = pl.pallas_call(
                functools.partial(step_kernel, count, spans, rows, cd_tiles, group),
                out_shape=(block, block),
                in_specs=[smem] + [vmem] * (1 + len(pieces) + len(parts)),
                out_specs=(vmem, vmem),
                scratch_shapes=[pltpu.VMEM((len(pieces) * spans * rows, slab), jnp.float32)],
                compiler_params=params,
                input_output_aliases={2 + len(pieces): 0, 3 + len(pieces): 1} if parts else {},
                cost_estimate=pl.CostEstimate(flops=1 << 30, bytes_accessed=4 << 20, transcendentals=0),
                name="step",
            )(listed, split, *pieces, *parts)
        mine, send = parts
        base = pl.pallas_call(
            merge_kernel,
            out_shape=pltpu.HBM((spans, half, slab), jnp.float32),
            in_specs=[vmem, vmem],
            out_specs=vmem,
            compiler_params=params,
            name="merge",
        )(mine, lax.ppermute(send, "cd", swap))

        last = pl.pallas_call(
            functools.partial(last_kernel, cd_tiles),
            out_shape=pltpu.VMEM((spans * rows, slab), jnp.float32),
            in_specs=[smem, vmem, vmem],
            out_specs=vmem,
            compiler_params=params,
            cost_estimate=pl.CostEstimate(flops=1 << 34, bytes_accessed=4 << 20, transcendentals=0),
            name="last",
        )(listed, split, held[0, far])
        return pl.pallas_call(
            functools.partial(final_kernel, count, spans, rows),
            out_shape=pltpu.HBM((spans, half, slab), jnp.float32),
            in_specs=[vmem, vmem, hbm],
            out_specs=hbm,
            scratch_shapes=[pltpu.VMEM((spans * rows, slab), jnp.float32), pltpu.SemaphoreType.DMA((spans,))],
            compiler_params=params,
            input_output_aliases={2: 0},
            name="final",
        )(last, lax.ppermute(last, "cd", swap), base)

    in_specs = (
        P("groups", "ab", "cd"),
        P(("groups", "ab"), "cd"),
        P(("groups", "ab")),
        P(("groups", "cd")),
        P(("groups", "ab"), "cd"),
    )
    out_specs = P("groups", "cd", "ab")
    return jax.shard_map(shards, mesh=mesh, in_specs=in_specs, out_specs=out_specs, check_vma=False)
```

time: 38.2 us -> 35.5 us (0.929); the launches traced: 38.3 us -> 34.9 us
  waiting for transfers between devices: 3.84 us -> 10 us
  starting transfers between devices: 18.7 us -> 13.4 us
  between operations: 2.71 us -> 0.06 us
  local copies, waits for them, and re-layouts: 1.73 us -> 0 us
  Pallas kernels: 10.4 us -> 11.4 us
  other arithmetic: 0.92 us -> 0 us
    ppermute x16 -> x9, waiting for transfers between devices: 3.84 us -> 10 us  [the longest x7 9.89 us: shards(): piece = lax.ppermute(piece, ('ab', 'cd'), around[chain])]
    ppermute x16 -> x9, starting transfers between devices: 18.7 us -> 13.4 us  [the longest x7 8.66 us: shards(): piece = lax.ppermute(piece, ('ab', 'cd'), around[chain])]
    slice x2 -> x0, local copies, waits for them, and re-layouts: 1.57 us -> none  [the longest x1 0.99 us: shards(): own = amplitudes[span:span + 1]]
    pallas_call x4 -> x7, Pallas kernels: 9.08 us -> 10.3 us  [the longest x4 5.16 us: shards(): pl.pallas_call(functools.partial(step_kernel, count, spans, rows, cd_tile...]
    select_n x1 -> x0, other arithmetic: 0.9 us -> none  [shards(): jnp.where(here, last.reshape(spans, 1, rows, slab), base.reshape(spans, f...]
  transfers between devices with their start and end apart: 16 -> 9, of which waited for: 3 -> 6; matrix products, arithmetic and copies ran while one was open for 2% -> 0% of each run, Pallas kernels for 27% -> 31%
where the time goes in v3:
time: 35.5 us; the launch traced here: 34.9 us
  starting transfers between devices  13.4 us (38%)
  Pallas kernels  11.4 us (32%)
  waiting for transfers between devices  10 us (28%)
    ppermute x7, waiting for transfers between devices, shards(): piece = lax.ppermute(piece, ('ab', 'cd'), around[chain])  9.89 us
    ppermute x7, starting transfers between devices, shards(): piece = lax.ppermute(piece, ('ab', 'cd'), around[chain])  8.66 us
    pallas_call x4, Pallas kernels, shards(): pl.pallas_call(functools.partial(step_kernel, count, spans, rows, cd_tile...  5.16 us
    ppermute x1, starting transfers between devices, shards(): lax.ppermute(send, 'cd', swap)  3.9 us
    pallas_call x1, Pallas kernels, shards(): pl.pallas_call(functools.partial(pick_kernel, ab_tiles, cd_tiles), out_sh...  3.61 us
    pallas_call x1, Pallas kernels, shards(): pl.pallas_call(functools.partial(last_kernel, cd_tiles), out_shape=pltpu....  1.12 us
    pallas_call x1, Pallas kernels, shards(): pl.pallas_call(merge_kernel, out_shape=pltpu.HBM((spans, half, slab), jnp...  0.87 us
    ppermute x1, starting transfers between devices, shards(): lax.ppermute(last, 'cd', swap)  0.8 us
  transfers between devices with their start and end apart: 9, of which 6 were waited for; matrix products, arithmetic and copies ran while one was open for 0% of the time, Pallas kernels for 31%

profile of v3, /device:TPU:1, one launch (start us, length us, event | category | flops | bytes accessed | tf_op | source)
XLA Modules:
  0.0 34.9 jit_solution(6283344483179586632)
XLA Ops:
  0.0 2.1 %collective-permute-start = (f32[2,16,2048]{2,1,0:T(8,128)}, f32[2,16,2048]{2,1,0:T(8,128)S(1)}, u32[]{:S(2)}, u32[]{:S(2)}) collective-permute-start(f32[2,16,2048]{2,1,0:T(8,128)} %amplitudes.1), channel_id=1, source_target_pairs={{0,4},{1,3},{4,8},{5,1},{8,12},{9,5},{12,14},{13,9},{14,10},{15,13... | collective-permute-start | bytes 786440 | tf_op jit(solution)/shard_map/ppermute | solution.py:235
  2.1 3.6 %pick.1 = (s32[133]{0:T(256)S(1)}, bf16[132,128,256]{2,1,0:T(8,128)(2,1)S(1)}, f32[2,16,2048]{2,1,0:T(8,128)S(1)}) custom-call(s32[8,16]{1,0:T(8,128)} %pattern.1, s32[8]{0:T(128)} %ab_irrep.1, s32[16]{0:T(128)} %cd_irrep.1, f32[1024,2048]{1,0:T(8,128)} %integrals.1, f32[2,16,2048]{2,1,0:T(8,128)} %amplitudes.1), custom_call_target="tpu_custom_call" | custom-call | bytes 8388608 | tf_op jit(solution)/shard_map/pick/pallas_call | solution.py:213
  5.7 0.6 %collective-permute-start.5 = (f32[2,16,2048]{2,1,0:T(8,128)S(1)}, f32[2,16,2048]{2,1,0:T(8,128)S(1)}, u32[]{:S(2)}, u32[]{:S(2)}) collective-permute-start(f32[2,16,2048]{2,1,0:T(8,128)S(1)} %get-tuple-element.18.refs_0_), channel_id=1, source_target_pairs={{0,2},{1,5},{4,0},{5,9},{8,4},{9,13},{12,8},{13,15},{14,12},{15,11... | collective-permute-start | bytes 786440 | tf_op jit(solution)/shard_map/ppermute | solution.py:235
  6.3 0.1 collective-permute-done.refs_1_
  6.4 1.4 %collective-permute-start.1 = (f32[2,16,2048]{2,1,0:T(8,128)S(1)}, f32[2,16,2048]{2,1,0:T(8,128)S(1)}, u32[]{:S(2)}, u32[]{:S(2)}) collective-permute-start(f32[2,16,2048]{2,1,0:T(8,128)S(1)} %collective-permute-done.refs_1_), channel_id=1, source_target_pairs={{0,4},{1,3},{4,8},{5,1},{8,12},{9,5},{12,14},{13,9},{14,10},{15,13... | collective-permute-start | bytes 786440 | tf_op jit(solution)/shard_map/ppermute | solution.py:235
  7.8 3.9 %collective-permute-done.5.refs_0_ = f32[2,16,2048]{2,1,0:T(8,128)S(1)} collective-permute-done((f32[2,16,2048]{2,1,0:T(8,128)S(1)}, f32[2,16,2048]{2,1,0:T(8,128)S(1)}, u32[]{:S(2)}, u32[]{:S(2)}) %collective-permute-start.5) | collective-permute-done | bytes 262176 | tf_op jit(solution)/shard_map/ppermute | solution.py:235
  11.7 0.0 collective-permute-start.6
  11.7 1.9 %collective-permute-done.1.refs_1_ = f32[2,16,2048]{2,1,0:T(8,128)S(1)} collective-permute-done((f32[2,16,2048]{2,1,0:T(8,128)S(1)}, f32[2,16,2048]{2,1,0:T(8,128)S(1)}, u32[]{:S(2)}, u32[]{:S(2)}) %collective-permute-start.1) | collective-permute-done | bytes 262176 | tf_op jit(solution)/shard_map/ppermute | solution.py:235
  13.6 1.6 %collective-permute-start.2 = (f32[2,16,2048]{2,1,0:T(8,128)S(1)}, f32[2,16,2048]{2,1,0:T(8,128)S(1)}, u32[]{:S(2)}, u32[]{:S(2)}) collective-permute-start(f32[2,16,2048]{2,1,0:T(8,128)S(1)} %collective-permute-done.1.refs_1_), channel_id=1, source_target_pairs={{0,4},{1,3},{4,8},{5,1},{8,12},{9,5},{12,14},{13,9},{14,10},{15,13... | collective-permute-start | bytes 786440 | tf_op jit(solution)/shard_map/ppermute | solution.py:235
  15.2 1.9 %collective-permute-done.6.refs_0_ = f32[2,16,2048]{2,1,0:T(8,128)S(1)} collective-permute-done((f32[2,16,2048]{2,1,0:T(8,128)S(1)}, f32[2,16,2048]{2,1,0:T(8,128)S(1)}, u32[]{:S(2)}, u32[]{:S(2)}) %collective-permute-start.6) | collective-permute-done | bytes 262176 | tf_op jit(solution)/shard_map/ppermute | solution.py:235
  17.1 0.7 %collective-permute-start.7 = (f32[2,16,2048]{2,1,0:T(8,128)S(1)}, f32[2,16,2048]{2,1,0:T(8,128)S(1)}, u32[]{:S(2)}, u32[]{:S(2)}) collective-permute-start(f32[2,16,2048]{2,1,0:T(8,128)S(1)} %collective-permute-done.6.refs_0_), channel_id=1, source_target_pairs={{0,2},{1,5},{4,0},{5,9},{8,4},{9,13},{12,8},{13,15},{14,12},{15,11... | collective-permute-start | bytes 786440 | tf_op jit(solution)/shard_map/ppermute | solution.py:235
  17.9 1.3 %step.4 = (f32[2,64,1024]{2,1,0:T(8,128)S(1)}, f32[2,64,1024]{2,1,0:T(8,128)S(1)}) custom-call(s32[133]{0:T(256)S(1)} %get-tuple-element.16.listed, bf16[132,128,256]{2,1,0:T(8,128)(2,1)S(1)} %get-tuple-element.17.split, f32[2,16,2048]{2,1,0:T(8,128)S(1)} %get-tuple-element.18.refs_0_, f32[2,16,2048]{2,1,0:T(8,128)S(1)} %collective-permute-done.refs_1_), custom_call_target="tpu_custom_call" | custom-call | flops 1073741824 | bytes 4194304 | tf_op jit(solution)/shard_map/step/pallas_call | solution.py:242
  19.2 2.1 %collective-permute-done.2.refs_1_ = f32[2,16,2048]{2,1,0:T(8,128)S(1)} collective-permute-done((f32[2,16,2048]{2,1,0:T(8,128)S(1)}, f32[2,16,2048]{2,1,0:T(8,128)S(1)}, u32[]{:S(2)}, u32[]{:S(2)}) %collective-permute-start.2) | collective-permute-done | bytes 262176 | tf_op jit(solution)/shard_map/ppermute | solution.py:235
  21.3 2.2 %collective-permute-start.3 = (f32[2,16,2048]{2,1,0:T(8,128)S(1)}, f32[2,16,2048]{2,1,0:T(8,128)S(1)}, u32[]{:S(2)}, u32[]{:S(2)}) collective-permute-start(f32[2,16,2048]{2,1,0:T(8,128)S(1)} %collective-permute-done.2.refs_1_), channel_id=1, source_target_pairs={{0,4},{1,3},{4,8},{5,1},{8,12},{9,5},{12,14},{13,9},{14,10},{15,13... | collective-permute-start | bytes 786440 | tf_op jit(solution)/shard_map/ppermute | solution.py:235
  23.5 1.3 %step.5 = (f32[2,64,1024]{2,1,0:T(8,128)S(1)}, f32[2,64,1024]{2,1,0:T(8,128)S(1)}) custom-call(s32[133]{0:T(256)S(1)} %get-tuple-element.16.listed, bf16[132,128,256]{2,1,0:T(8,128)(2,1)S(1)} %get-tuple-element.17.split, f32[2,16,2048]{2,1,0:T(8,128)S(1)} %collective-permute-done.5.refs_0_, ...), custom_call_target="tpu_custom_call", output_to_operand_aliasing={{0}: (4, {}), {1}: (5, {})} | custom-call | flops 1073741824 | bytes 4194304 | tf_op jit(solution)/shard_map/step/pallas_call | solution.py:242
  24.8 1.3 %step.6 = (f32[2,64,1024]{2,1,0:T(8,128)S(1)}, f32[2,64,1024]{2,1,0:T(8,128)S(1)}) custom-call(s32[133]{0:T(256)S(1)} %get-tuple-element.16.listed, bf16[132,128,256]{2,1,0:T(8,128)(2,1)S(1)} %get-tuple-element.17.split, f32[2,16,2048]{2,1,0:T(8,128)S(1)} %collective-permute-done.6.refs_0_, ...), custom_call_target="tpu_custom_call", output_to_operand_aliasing={{0}: (4, {}), {1}: (5, {})} | custom-call | flops 1073741824 | bytes 4194304 | tf_op jit(solution)/shard_map/step/pallas_call | solution.py:242
  26.2 0.0 collective-permute-done.7.refs_0_
  26.2 1.2 %step.7 = (f32[2,64,1024]{2,1,0:T(8,128)S(1)}, f32[2,64,1024]{2,1,0:T(8,128)S(1)}) custom-call(s32[133]{0:T(256)S(1)} %get-tuple-element.16.listed, bf16[132,128,256]{2,1,0:T(8,128)(2,1)S(1)} %get-tuple-element.17.split, f32[2,16,2048]{2,1,0:T(8,128)S(1)} %collective-permute-done.7.refs_0_, ...), custom_call_target="tpu_custom_call", output_to_operand_aliasing={{0}: (3, {}), {1}: (4, {})} | custom-call | flops 1073741824 | bytes 4194304 | tf_op jit(solution)/shard_map/step/pallas_call | solution.py:242
  27.4 3.9 %collective-permute-start.8 = (f32[2,64,1024]{2,1,0:T(8,128)S(1)}, f32[2,64,1024]{2,1,0:T(8,128)S(1)}, u32[]{:S(2)}, u32[]{:S(2)}) collective-permute-start(f32[2,64,1024]{2,1,0:T(8,128)S(1)} %get-tuple-element.26), channel_id=1, source_target_pairs={{0,1},{1,0},{2,3},{3,2},{4,5},{5,4},{6,7},{7,6},{8,9},{9,8},{10,11... | collective-permute-start | bytes 1572872 | tf_op jit(solution)/shard_map/ppermute | solution.py:261
  31.3 0.0 collective-permute-done.3.piece
  31.3 1.1 %last.1 = f32[32,1024]{1,0:T(8,128)S(1)} custom-call(s32[133]{0:T(256)S(1)} %get-tuple-element.16.listed, bf16[132,128,256]{2,1,0:T(8,128)(2,1)S(1)} %get-tuple-element.17.split, f32[2,16,2048]{2,1,0:T(8,128)S(1)} %collective-permute-done.3.piece), custom_call_target="tpu_custom_call" | custom-call | flops 17179869184 | bytes 4194304 | tf_op jit(solution)/shard_map/last/pallas_call | solution.py:263
  32.4 0.8 %collective-permute-start.4 = (f32[32,1024]{1,0:T(8,128)S(1)}, f32[32,1024]{1,0:T(8,128)S(1)}, u32[]{:S(2)}, u32[]{:S(2)}) collective-permute-start(f32[32,1024]{1,0:T(8,128)S(1)} %last.1), channel_id=1, source_target_pairs={{0,1},{1,0},{2,3},{3,2},{4,5},{5,4},{6,7},{7,6},{8,9},{9,8},{10,11... | collective-permute-start | bytes 393224 | tf_op jit(solution)/shard_map/ppermute | solution.py:281
  33.2 0.0 collective-permute-done.8.received
  33.2 0.9 %merge.1.before = f32[2,64,1024]{2,1,0:T(8,128)} custom-call(f32[2,64,1024]{2,1,0:T(8,128)S(1)} %get-tuple-element.25.mine, f32[2,64,1024]{2,1,0:T(8,128)S(1)} %collective-permute-done.8.received), custom_call_target="tpu_custom_call" | custom-call | tf_op jit(solution)/shard_map/merge/pallas_call | solution.py:254
  34.1 0.1 collective-permute-done.4.received
  34.2 0.7 %final.1 = f32[2,64,1024]{2,1,0:T(8,128)} custom-call(f32[32,1024]{1,0:T(8,128)S(1)} %last.1, f32[32,1024]{1,0:T(8,128)S(1)} %collective-permute-done.4.received, f32[2,64,1024]{2,1,0:T(8,128)} %merge.1.before), custom_call_target="tpu_custom_call", output_to_operand_aliasing={{}: (2, {})} | custom-call | tf_op jit(solution)/shard_map/final/pallas_call | solution.py:272
Async XLA Ops:
  0.0 6.4 %collective-permute-start = (f32[2,16,2048]{2,1,0:T(8,128)}, f32[2,16,2048]{2,1,0:T(8,128)S(1)}, u32[]{:S(2)}, u32[]{:S(2)}) collective-permute-start(f32[2,16,2048]{2,1,0:T(8,128)} %amplitudes.1), channel_id=1, source_target_pairs={{0,4},{1,3},{4,8},{5,1},{8,12},{9,5},{12,14},{13,9},{14,10},{15,13... | collective-permute-start | bytes 786440 | tf_op jit(solution)/shard_map/ppermute | solution.py:235
  5.7 6.0 %collective-permute-start.5 = (f32[2,16,2048]{2,1,0:T(8,128)S(1)}, f32[2,16,2048]{2,1,0:T(8,128)S(1)}, u32[]{:S(2)}, u32[]{:S(2)}) collective-permute-start(f32[2,16,2048]{2,1,0:T(8,128)S(1)} %get-tuple-element.18.refs_0_), channel_id=1, source_target_pairs={{0,2},{1,5},{4,0},{5,9},{8,4},{9,13},{12,8},{13,15},{14,12},{15,11... | collective-permute-start | bytes 786440 | tf_op jit(solution)/shard_map/ppermute | solution.py:235
  6.4 7.2 %collective-permute-start.1 = (f32[2,16,2048]{2,1,0:T(8,128)S(1)}, f32[2,16,2048]{2,1,0:T(8,128)S(1)}, u32[]{:S(2)}, u32[]{:S(2)}) collective-permute-start(f32[2,16,2048]{2,1,0:T(8,128)S(1)} %collective-permute-done.refs_1_), channel_id=1, source_target_pairs={{0,4},{1,3},{4,8},{5,1},{8,12},{9,5},{12,14},{13,9},{14,10},{15,13... | collective-permute-start | bytes 786440 | tf_op jit(solution)/shard_map/ppermute | solution.py:235
  11.7 5.5 %collective-permute-start.6 = (f32[2,16,2048]{2,1,0:T(8,128)S(1)}, f32[2,16,2048]{2,1,0:T(8,128)S(1)}, u32[]{:S(2)}, u32[]{:S(2)}) collective-permute-start(f32[2,16,2048]{2,1,0:T(8,128)S(1)} %collective-permute-done.5.refs_0_), channel_id=1, source_target_pairs={{0,2},{1,5},{4,0},{5,9},{8,4},{9,13},{12,8},{13,15},{14,12},{15,11... | collective-permute-start | bytes 786440 | tf_op jit(solution)/shard_map/ppermute | solution.py:235
  13.6 7.7 %collective-permute-start.2 = (f32[2,16,2048]{2,1,0:T(8,128)S(1)}, f32[2,16,2048]{2,1,0:T(8,128)S(1)}, u32[]{:S(2)}, u32[]{:S(2)}) collective-permute-start(f32[2,16,2048]{2,1,0:T(8,128)S(1)} %collective-permute-done.1.refs_1_), channel_id=1, source_target_pairs={{0,4},{1,3},{4,8},{5,1},{8,12},{9,5},{12,14},{13,9},{14,10},{15,13... | collective-permute-start | bytes 786440 | tf_op jit(solution)/shard_map/ppermute | solution.py:235
  17.1 9.0 %collective-permute-start.7 = (f32[2,16,2048]{2,1,0:T(8,128)S(1)}, f32[2,16,2048]{2,1,0:T(8,128)S(1)}, u32[]{:S(2)}, u32[]{:S(2)}) collective-permute-start(f32[2,16,2048]{2,1,0:T(8,128)S(1)} %collective-permute-done.6.refs_0_), channel_id=1, source_target_pairs={{0,2},{1,5},{4,0},{5,9},{8,4},{9,13},{12,8},{13,15},{14,12},{15,11... | collective-permute-start | bytes 786440 | tf_op jit(solution)/shard_map/ppermute | solution.py:235
  21.3 10.0 %collective-permute-start.3 = (f32[2,16,2048]{2,1,0:T(8,128)S(1)}, f32[2,16,2048]{2,1,0:T(8,128)S(1)}, u32[]{:S(2)}, u32[]{:S(2)}) collective-permute-start(f32[2,16,2048]{2,1,0:T(8,128)S(1)} %collective-permute-done.2.refs_1_), channel_id=1, source_target_pairs={{0,4},{1,3},{4,8},{5,1},{8,12},{9,5},{12,14},{13,9},{14,10},{15,13... | collective-permute-start | bytes 786440 | tf_op jit(solution)/shard_map/ppermute | solution.py:235
  27.4 5.8 %collective-permute-start.8 = (f32[2,64,1024]{2,1,0:T(8,128)S(1)}, f32[2,64,1024]{2,1,0:T(8,128)S(1)}, u32[]{:S(2)}, u32[]{:S(2)}) collective-permute-start(f32[2,64,1024]{2,1,0:T(8,128)S(1)} %get-tuple-element.26), channel_id=1, source_target_pairs={{0,1},{1,0},{2,3},{3,2},{4,5},{5,4},{6,7},{7,6},{8,9},{9,8},{10,11... | collective-permute-start | bytes 1572872 | tf_op jit(solution)/shard_map/ppermute | solution.py:261
  32.4 1.8 %collective-permute-start.4 = (f32[32,1024]{1,0:T(8,128)S(1)}, f32[32,1024]{1,0:T(8,128)S(1)}, u32[]{:S(2)}, u32[]{:S(2)}) collective-permute-start(f32[32,1024]{1,0:T(8,128)S(1)} %last.1), channel_id=1, source_target_pairs={{0,1},{1,0},{2,3},{3,2},{4,5},{5,4},{6,7},{7,6},{8,9},{9,8},{10,11... | collective-permute-start | bytes 393224 | tf_op jit(solution)/shard_map/ppermute | solution.py:281

commit v4 on v3

--- a/solution.py
+++ b/solution.py
@@ -10,6 +10,7 @@
 TILE = 128
 UNROLL = 4
 FLIGHT = 32
+GROUP = 4
 VMEM_LIMIT = 12 * 2**20
 
 
@@ -93,14 +94,14 @@
     listed[0] = found
     for extra in range(UNROLL):
         listed[1 + found + extra] = 0
-        split[found + extra] = jnp.zeros((TILE, 2 * TILE), jnp.bfloat16)
+        split[found + extra] = jnp.zeros((2 * TILE, TILE), jnp.bfloat16)
 
     def part(k, carry):
         fetch(k).wait()
-        tile = landed[k % FLIGHT].T
+        tile = landed[k % FLIGHT]
         upper = tile.astype(jnp.bfloat16)
-        split[k, :, :TILE] = upper
-        split[k, :, TILE:] = (tile - upper.astype(jnp.float32)).astype(jnp.bfloat16)
+        split[k, :TILE] = upper
+        split[k, TILE:] = (tile - upper.astype(jnp.float32)).astype(jnp.bfloat16)
 
         @pl.when(k + FLIGHT < found)
         def _():
@@ -116,6 +117,7 @@
     total[...] = jnp.zeros_like(total)
 
     def step(round_at, carry):
+        sums = []
         for unrolled in range(UNROLL):
             k = round_at * UNROLL + unrolled
             tile = listed[1 + k]
@@ -125,10 +127,16 @@
             left = jnp.concatenate([piece[span, :, columns] for piece in pieces for span in range(piece.shape[0])], axis=0)
             upper = left.astype(jnp.bfloat16)
             lower = (left - upper.astype(jnp.float32)).astype(jnp.bfloat16)
-            both = jnp.dot(jnp.concatenate([upper, lower], axis=0), split[k], preferred_element_type=jnp.float32)
+            both = lax.dot_general(
+                jnp.concatenate([upper, lower], axis=0),
+                split[k],
+                (((1,), (1,)), ((), ())),
+                preferred_element_type=jnp.float32,
+            )
             high, low = both[: left.shape[0]], both[left.shape[0] :]
-            into = pl.ds(pl.multiple_of(p * TILE, TILE), TILE)
-            total[:, into] += high[:, :TILE] + (high[:, TILE:] + (low[:, :TILE] + low[:, TILE:]))
+            sums.append((p, high[:, :TILE] + (high[:, TILE:] + (low[:, :TILE] + low[:, TILE:]))))
+        for p, term in sums:
+            total[:, pl.ds(pl.multiple_of(p * TILE, TILE), TILE)] += term
         return carry
 
     lax.fori_loop(0, (listed[0] + UNROLL - 1) // UNROLL, step, 0)
@@ -214,7 +222,7 @@
             functools.partial(pick_kernel, ab_tiles, cd_tiles),
             out_shape=(
                 jax.ShapeDtypeStruct((1 + tiles + UNROLL,), jnp.int32),
-                pltpu.VMEM((tiles + UNROLL, TILE, 2 * TILE), jnp.bfloat16),
+                pltpu.VMEM((tiles + UNROLL, 2 * TILE, TILE), jnp.bfloat16),
                 pltpu.VMEM(amplitudes.shape, jnp.float32),
             ),
             in_specs=[smem, smem, smem, hbm, hbm],
@@ -237,7 +245,9 @@
 
         block = pltpu.VMEM((spans, half, slab), jnp.float32)
         parts = ()
-        for group in [[(0, 0), (0, 1)]] + [[(1, hop - 1), (0, hop)] for hop in range(2, far)] + [[(1, far - 1)]]:
+        arrivals = [(0, 0)] + [(chain, hop) for hop in range(1, far) for chain in range(2)]
+        for at in range(0, len(arrivals), GROUP):
+            group = arrivals[at : at + GROUP]
             pieces = [held[chunk] for chunk in group]
             parts = pl.pallas_call(
                 functools.partial(step_kernel, count, spans, rows, cd_tiles, group),

time: 35.5 us -> 36 us (1.014)
  Pallas kernels: 11.4 us -> 9.17 us
  starting transfers between devices: 13.4 us -> 15 us
  waiting for transfers between devices: 10 us -> 11.4 us
    ppermute x1, starting transfers between devices: 3.9 us -> 5.99 us  [shards(): lax.ppermute(send, 'cd', swap)]
    pallas_call x4 -> x2, Pallas kernels: 5.16 us -> 3.2 us  [shards(): pl.pallas_call(functools.partial(step_kernel, count, spans, rows, cd_tile...]
    ppermute x7, waiting for transfers between devices: 9.89 us -> 11.1 us  [shards(): piece = lax.ppermute(piece, ('ab', 'cd'), around[chain])]
    ppermute x1, starting transfers between devices: 0.8 us -> 0.31 us  [shards(): lax.ppermute(last, 'cd', swap)]
    pallas_call x1, Pallas kernels: 3.61 us -> 3.22 us  [shards(): pl.pallas_call(functools.partial(pick_kernel, ab_tiles, cd_tiles), out_sh...]
  transfers between devices with their start and end apart: 9 -> 9, of which waited for: 6 -> 6; matrix products, arithmetic and copies ran while one was open for 0% -> 0% of each run, Pallas kernels for 31% -> 24%
where the time goes in v4:
time: 36 us; the launch traced here: 35.5 us
  starting transfers between devices  15 us (42%)
  waiting for transfers between devices  11.4 us (32%)
  Pallas kernels  9.17 us (25%)
    ppermute x7, waiting for transfers between devices, shards(): piece = lax.ppermute(piece, ('ab', 'cd'), around[chain])  11.1 us
    ppermute x7, starting transfers between devices, shards(): piece = lax.ppermute(piece, ('ab', 'cd'), around[chain])  8.67 us
    ppermute x1, starting transfers between devices, shards(): lax.ppermute(send, 'cd', swap)  5.99 us
    pallas_call x1, Pallas kernels, shards(): pl.pallas_call(functools.partial(pick_kernel, ab_tiles, cd_tiles), out_sh...  3.22 us
    pallas_call x2, Pallas kernels, shards(): pl.pallas_call(functools.partial(step_kernel, count, spans, rows, cd_tile...  3.2 us
    pallas_call x1, Pallas kernels, shards(): pl.pallas_call(functools.partial(last_kernel, cd_tiles), out_shape=pltpu....  1.21 us
    pallas_call x1, Pallas kernels, shards(): pl.pallas_call(merge_kernel, out_shape=pltpu.HBM((spans, half, slab), jnp...  0.87 us
  transfers between devices with their start and end apart: 9, of which 6 were waited for; matrix products, arithmetic and copies ran while one was open for 0% of the time, Pallas kernels for 24%

profile of v4, /device:TPU:1, one launch (start us, length us, event | category | flops | bytes accessed | tf_op | source)
XLA Modules:
  0.0 35.5 jit_solution(17553457858695803508)
XLA Ops:
  0.0 2.1 %collective-permute-start = (f32[2,16,2048]{2,1,0:T(8,128)}, f32[2,16,2048]{2,1,0:T(8,128)S(1)}, u32[]{:S(2)}, u32[]{:S(2)}) collective-permute-start(f32[2,16,2048]{2,1,0:T(8,128)} %amplitudes.1), channel_id=1, source_target_pairs={{0,4},{1,3},{4,8},{5,1},{8,12},{9,5},{12,14},{13,9},{14,10},{15,13... | collective-permute-start | bytes 786440 | tf_op jit(solution)/shard_map/ppermute | solution.py:243
  2.1 3.2 %pick.1 = (s32[133]{0:T(256)S(1)}, bf16[132,256,128]{2,1,0:T(8,128)(2,1)S(1)}, f32[2,16,2048]{2,1,0:T(8,128)S(1)}) custom-call(s32[8,16]{1,0:T(8,128)} %pattern.1, s32[8]{0:T(128)} %ab_irrep.1, s32[16]{0:T(128)} %cd_irrep.1, f32[1024,2048]{1,0:T(8,128)} %integrals.1, f32[2,16,2048]{2,1,0:T(8,128)} %amplitudes.1), custom_call_target="tpu_custom_call" | custom-call | bytes 8388608 | tf_op jit(solution)/shard_map/pick/pallas_call | solution.py:221
  5.3 0.2 collective-permute-start.5
  5.5 0.9 %collective-permute-done.refs_1_ = f32[2,16,2048]{2,1,0:T(8,128)S(1)} collective-permute-done((f32[2,16,2048]{2,1,0:T(8,128)}, f32[2,16,2048]{2,1,0:T(8,128)S(1)}, u32[]{:S(2)}, u32[]{:S(2)}) %collective-permute-start) | collective-permute-done | bytes 262176 | tf_op jit(solution)/shard_map/ppermute | solution.py:243
  6.4 1.4 %collective-permute-start.1 = (f32[2,16,2048]{2,1,0:T(8,128)S(1)}, f32[2,16,2048]{2,1,0:T(8,128)S(1)}, u32[]{:S(2)}, u32[]{:S(2)}) collective-permute-start(f32[2,16,2048]{2,1,0:T(8,128)S(1)} %collective-permute-done.refs_1_), channel_id=1, source_target_pairs={{0,4},{1,3},{4,8},{5,1},{8,12},{9,5},{12,14},{13,9},{14,10},{15,13... | collective-permute-start | bytes 786440 | tf_op jit(solution)/shard_map/ppermute | solution.py:243
  7.8 3.1 %collective-permute-done.5.refs_2_ = f32[2,16,2048]{2,1,0:T(8,128)S(1)} collective-permute-done((f32[2,16,2048]{2,1,0:T(8,128)S(1)}, f32[2,16,2048]{2,1,0:T(8,128)S(1)}, u32[]{:S(2)}, u32[]{:S(2)}) %collective-permute-start.5) | collective-permute-done | bytes 262176 | tf_op jit(solution)/shard_map/ppermute | solution.py:243
  10.9 0.9 %collective-permute-start.6 = (f32[2,16,2048]{2,1,0:T(8,128)S(1)}, f32[2,16,2048]{2,1,0:T(8,128)S(1)}, u32[]{:S(2)}, u32[]{:S(2)}) collective-permute-start(f32[2,16,2048]{2,1,0:T(8,128)S(1)} %collective-permute-done.5.refs_2_), channel_id=1, source_target_pairs={{0,2},{1,5},{4,0},{5,9},{8,4},{9,13},{12,8},{13,15},{14,12},{15,11... | collective-permute-start | bytes 786440 | tf_op jit(solution)/shard_map/ppermute | solution.py:243
  11.8 2.5 %collective-permute-done.1.refs_3_ = f32[2,16,2048]{2,1,0:T(8,128)S(1)} collective-permute-done((f32[2,16,2048]{2,1,0:T(8,128)S(1)}, f32[2,16,2048]{2,1,0:T(8,128)S(1)}, u32[]{:S(2)}, u32[]{:S(2)}) %collective-permute-start.1) | collective-permute-done | bytes 262176 | tf_op jit(solution)/shard_map/ppermute | solution.py:243
  14.3 0.7 %collective-permute-start.2 = (f32[2,16,2048]{2,1,0:T(8,128)S(1)}, f32[2,16,2048]{2,1,0:T(8,128)S(1)}, u32[]{:S(2)}, u32[]{:S(2)}) collective-permute-start(f32[2,16,2048]{2,1,0:T(8,128)S(1)} %collective-permute-done.1.refs_3_), channel_id=1, source_target_pairs={{0,4},{1,3},{4,8},{5,1},{8,12},{9,5},{12,14},{13,9},{14,10},{15,13... | collective-permute-start | bytes 786440 | tf_op jit(solution)/shard_map/ppermute | solution.py:243
  15.0 1.7 %collective-permute-done.6.refs_0_ = f32[2,16,2048]{2,1,0:T(8,128)S(1)} collective-permute-done((f32[2,16,2048]{2,1,0:T(8,128)S(1)}, f32[2,16,2048]{2,1,0:T(8,128)S(1)}, u32[]{:S(2)}, u32[]{:S(2)}) %collective-permute-start.6) | collective-permute-done | bytes 262176 | tf_op jit(solution)/shard_map/ppermute | solution.py:243
  16.7 1.9 %collective-permute-start.7 = (f32[2,16,2048]{2,1,0:T(8,128)S(1)}, f32[2,16,2048]{2,1,0:T(8,128)S(1)}, u32[]{:S(2)}, u32[]{:S(2)}) collective-permute-start(f32[2,16,2048]{2,1,0:T(8,128)S(1)} %collective-permute-done.6.refs_0_), channel_id=1, source_target_pairs={{0,2},{1,5},{4,0},{5,9},{8,4},{9,13},{12,8},{13,15},{14,12},{15,11... | collective-permute-start | bytes 786440 | tf_op jit(solution)/shard_map/ppermute | solution.py:243
  18.6 3.0 %collective-permute-done.2.refs_1_ = f32[2,16,2048]{2,1,0:T(8,128)S(1)} collective-permute-done((f32[2,16,2048]{2,1,0:T(8,128)S(1)}, f32[2,16,2048]{2,1,0:T(8,128)S(1)}, u32[]{:S(2)}, u32[]{:S(2)}) %collective-permute-start.2) | collective-permute-done | bytes 262176 | tf_op jit(solution)/shard_map/ppermute | solution.py:243
  21.6 1.4 %collective-permute-start.3 = (f32[2,16,2048]{2,1,0:T(8,128)S(1)}, f32[2,16,2048]{2,1,0:T(8,128)S(1)}, u32[]{:S(2)}, u32[]{:S(2)}) collective-permute-start(f32[2,16,2048]{2,1,0:T(8,128)S(1)} %collective-permute-done.2.refs_1_), channel_id=1, source_target_pairs={{0,4},{1,3},{4,8},{5,1},{8,12},{9,5},{12,14},{13,9},{14,10},{15,13... | collective-permute-start | bytes 786440 | tf_op jit(solution)/shard_map/ppermute | solution.py:243
  23.0 1.7 %step.2 = (f32[2,64,1024]{2,1,0:T(8,128)S(1)}, f32[2,64,1024]{2,1,0:T(8,128)S(1)}) custom-call(s32[133]{0:T(256)S(1)} %get-tuple-element.12.listed, bf16[132,256,128]{2,1,0:T(8,128)(2,1)S(1)} %get-tuple-element.13.split, f32[2,16,2048]{2,1,0:T(8,128)S(1)} %get-tuple-element.14.refs_0_, f32[2,16,2048]{2,1,0:T(8,128)S(1)} %collective-permute-done.refs_1_, ...), custom_call_target="tpu_custom_call" | custom-call | flops 1073741824 | bytes 4194304 | tf_op jit(solution)/shard_map/step/pallas_call | solution.py:252
  24.7 0.0 collective-permute-done.7.refs_2_
  24.7 1.5 %step.3 = (f32[2,64,1024]{2,1,0:T(8,128)S(1)}, f32[2,64,1024]{2,1,0:T(8,128)S(1)}) custom-call(s32[133]{0:T(256)S(1)} %get-tuple-element.12.listed, bf16[132,256,128]{2,1,0:T(8,128)(2,1)S(1)} %get-tuple-element.13.split, f32[2,16,2048]{2,1,0:T(8,128)S(1)} %collective-permute-done.6.refs_0_, ...), custom_call_target="tpu_custom_call", output_to_operand_aliasing={{0}: (5, {}), {1}: (6, {})} | custom-call | flops 1073741824 | bytes 4194304 | tf_op jit(solution)/shard_map/step/pallas_call | solution.py:252
  26.2 6.0 %collective-permute-start.8 = (f32[2,64,1024]{2,1,0:T(8,128)S(1)}, f32[2,64,1024]{2,1,0:T(8,128)S(1)}, u32[]{:S(2)}, u32[]{:S(2)}) collective-permute-start(f32[2,64,1024]{2,1,0:T(8,128)S(1)} %get-tuple-element.18), channel_id=1, source_target_pairs={{0,1},{1,0},{2,3},{3,2},{4,5},{5,4},{6,7},{7,6},{8,9},{9,8},{10,11... | collective-permute-start | bytes 1572872 | tf_op jit(solution)/shard_map/ppermute | solution.py:271
  32.2 0.0 collective-permute-done.3.piece
  32.2 1.2 %last.1 = f32[32,1024]{1,0:T(8,128)S(1)} custom-call(s32[133]{0:T(256)S(1)} %get-tuple-element.12.listed, bf16[132,256,128]{2,1,0:T(8,128)(2,1)S(1)} %get-tuple-element.13.split, f32[2,16,2048]{2,1,0:T(8,128)S(1)} %collective-permute-done.3.piece), custom_call_target="tpu_custom_call" | custom-call | flops 17179869184 | bytes 4194304 | tf_op jit(solution)/shard_map/last/pallas_call | solution.py:273
  33.4 0.3 collective-permute-start.4
  33.8 0.0 collective-permute-done.8.received
  33.8 0.9 %merge.1.before = f32[2,64,1024]{2,1,0:T(8,128)} custom-call(f32[2,64,1024]{2,1,0:T(8,128)S(1)} %get-tuple-element.17.mine, f32[2,64,1024]{2,1,0:T(8,128)S(1)} %collective-permute-done.8.received), custom_call_target="tpu_custom_call" | custom-call | tf_op jit(solution)/shard_map/merge/pallas_call | solution.py:264
  34.6 0.2 collective-permute-done.4.received
  34.9 0.7 %final.1 = f32[2,64,1024]{2,1,0:T(8,128)} custom-call(f32[32,1024]{1,0:T(8,128)S(1)} %last.1, f32[32,1024]{1,0:T(8,128)S(1)} %collective-permute-done.4.received, f32[2,64,1024]{2,1,0:T(8,128)} %merge.1.before), custom_call_target="tpu_custom_call", output_to_operand_aliasing={{}: (2, {})} | custom-call | tf_op jit(solution)/shard_map/final/pallas_call | solution.py:282
Async XLA Ops:
  0.0 6.4 %collective-permute-start = (f32[2,16,2048]{2,1,0:T(8,128)}, f32[2,16,2048]{2,1,0:T(8,128)S(1)}, u32[]{:S(2)}, u32[]{:S(2)}) collective-permute-start(f32[2,16,2048]{2,1,0:T(8,128)} %amplitudes.1), channel_id=1, source_target_pairs={{0,4},{1,3},{4,8},{5,1},{8,12},{9,5},{12,14},{13,9},{14,10},{15,13... | collective-permute-start | bytes 786440 | tf_op jit(solution)/shard_map/ppermute | solution.py:243
  5.3 5.6 %collective-permute-start.5 = (f32[2,16,2048]{2,1,0:T(8,128)S(1)}, f32[2,16,2048]{2,1,0:T(8,128)S(1)}, u32[]{:S(2)}, u32[]{:S(2)}) collective-permute-start(f32[2,16,2048]{2,1,0:T(8,128)S(1)} %get-tuple-element.14.refs_0_), channel_id=1, source_target_pairs={{0,2},{1,5},{4,0},{5,9},{8,4},{9,13},{12,8},{13,15},{14,12},{15,11... | collective-permute-start | bytes 786440 | tf_op jit(solution)/shard_map/ppermute | solution.py:243
  6.4 7.9 %collective-permute-start.1 = (f32[2,16,2048]{2,1,0:T(8,128)S(1)}, f32[2,16,2048]{2,1,0:T(8,128)S(1)}, u32[]{:S(2)}, u32[]{:S(2)}) collective-permute-start(f32[2,16,2048]{2,1,0:T(8,128)S(1)} %collective-permute-done.refs_1_), channel_id=1, source_target_pairs={{0,4},{1,3},{4,8},{5,1},{8,12},{9,5},{12,14},{13,9},{14,10},{15,13... | collective-permute-start | bytes 786440 | tf_op jit(solution)/shard_map/ppermute | solution.py:243
  10.9 5.8 %collective-permute-start.6 = (f32[2,16,2048]{2,1,0:T(8,128)S(1)}, f32[2,16,2048]{2,1,0:T(8,128)S(1)}, u32[]{:S(2)}, u32[]{:S(2)}) collective-permute-start(f32[2,16,2048]{2,1,0:T(8,128)S(1)} %collective-permute-done.5.refs_2_), channel_id=1, source_target_pairs={{0,2},{1,5},{4,0},{5,9},{8,4},{9,13},{12,8},{13,15},{14,12},{15,11... | collective-permute-start | bytes 786440 | tf_op jit(solution)/shard_map/ppermute | solution.py:243
  14.3 7.4 %collective-permute-start.2 = (f32[2,16,2048]{2,1,0:T(8,128)S(1)}, f32[2,16,2048]{2,1,0:T(8,128)S(1)}, u32[]{:S(2)}, u32[]{:S(2)}) collective-permute-start(f32[2,16,2048]{2,1,0:T(8,128)S(1)} %collective-permute-done.1.refs_3_), channel_id=1, source_target_pairs={{0,4},{1,3},{4,8},{5,1},{8,12},{9,5},{12,14},{13,9},{14,10},{15,13... | collective-permute-start | bytes 786440 | tf_op jit(solution)/shard_map/ppermute | solution.py:243
  16.7 8.0 %collective-permute-start.7 = (f32[2,16,2048]{2,1,0:T(8,128)S(1)}, f32[2,16,2048]{2,1,0:T(8,128)S(1)}, u32[]{:S(2)}, u32[]{:S(2)}) collective-permute-start(f32[2,16,2048]{2,1,0:T(8,128)S(1)} %collective-permute-done.6.refs_0_), channel_id=1, source_target_pairs={{0,2},{1,5},{4,0},{5,9},{8,4},{9,13},{12,8},{13,15},{14,12},{15,11... | collective-permute-start | bytes 786440 | tf_op jit(solution)/shard_map/ppermute | solution.py:243
  21.6 10.6 %collective-permute-start.3 = (f32[2,16,2048]{2,1,0:T(8,128)S(1)}, f32[2,16,2048]{2,1,0:T(8,128)S(1)}, u32[]{:S(2)}, u32[]{:S(2)}) collective-permute-start(f32[2,16,2048]{2,1,0:T(8,128)S(1)} %collective-permute-done.2.refs_1_), channel_id=1, source_target_pairs={{0,4},{1,3},{4,8},{5,1},{8,12},{9,5},{12,14},{13,9},{14,10},{15,13... | collective-permute-start | bytes 786440 | tf_op jit(solution)/shard_map/ppermute | solution.py:243
  26.2 7.5 %collective-permute-start.8 = (f32[2,64,1024]{2,1,0:T(8,128)S(1)}, f32[2,64,1024]{2,1,0:T(8,128)S(1)}, u32[]{:S(2)}, u32[]{:S(2)}) collective-permute-start(f32[2,64,1024]{2,1,0:T(8,128)S(1)} %get-tuple-element.18), channel_id=1, source_target_pairs={{0,1},{1,0},{2,3},{3,2},{4,5},{5,4},{6,7},{7,6},{8,9},{9,8},{10,11... | collective-permute-start | bytes 1572872 | tf_op jit(solution)/shard_map/ppermute | solution.py:271
  33.4 1.4 %collective-permute-start.4 = (f32[32,1024]{1,0:T(8,128)S(1)}, f32[32,1024]{1,0:T(8,128)S(1)}, u32[]{:S(2)}, u32[]{:S(2)}) collective-permute-start(f32[32,1024]{1,0:T(8,128)S(1)} %last.1), channel_id=1, source_target_pairs={{0,1},{1,0},{2,3},{3,2},{4,5},{5,4},{6,7},{7,6},{8,9},{9,8},{10,11... | collective-permute-start | bytes 393224 | tf_op jit(solution)/shard_map/ppermute | solution.py:291
